TPU v7x, 128 devices: a whole 4x4x4 slice. The times are simulated.
128 devices in a mesh: tx: 8 (over x, core), ty: 16 (over z, y).
Axes of the slice: x: 4, y: 4, z: 4, core: 2. Of those that a mesh axis runs over, the one named last changes fastest.
Arguments:
- features: bfloat16 [512, 64, 512], P(('tx', 'ty')), may hold values from -6 to 6
- weights: bfloat16 [3, 27, 64, 64], replicated, may hold values from -0.4375 to 0.4375
- cotangent: bfloat16 [512, 64, 512], P(('tx', 'ty')), may hold values from -6 to 6
- neighbours: int32 [512, 27], P(('tx', 'ty')), may hold values from -1 to 511, as said below
Outputs:
- out: bfloat16 [512, 64, 512], P(('tx', 'ty'))
- weight_grads: float32 [3, 27, 64, 64], replicated
Inputs may be any that keep to these rules, and one draw needn't show every extreme that they name: `neighbours`: blocks lie on a grid of 16 x 2 * 16 x 2 block positions. The device at (r, c) of the tx x ty mesh holds slots from (r * 16 + c) * 4 on, placed at distinct positions whose first two coordinates lie in [2r, 2r+2) x [2c, 2c+2). A device's live slots come first. Devices (r, c) and (r, (c + 8) mod 16) are partners: in each pair one holds at most 2 live slots. Some device holds 4 live slots and its partner exactly 2.
All inputs are finite; a program needn't handle non-finite values.
Results may differ from a plain program's by a relative error of at most 0.013.
Values may be sent and summed in bfloat16 or wider, within the bound.
A program may use at most 128 MiB of HBM per device.

v0:
```python
import math

import jax
import jax.numpy as jnp
from jax import lax
from jax.sharding import PartitionSpec as P

BLK = 8
LAYERS = 3


def padded_2(shard, sides, width):
    for axis, dim in sides:
        peers, length = (lax.axis_size(axis), shard.shape[dim])
        up = [(i, (i + 1) % peers) for i in range(peers - 1)]
        down = [(j, i) for i, j in up]
        last = lax.slice_in_dim(shard, length - width, length, axis=dim)
        first = lax.slice_in_dim(shard, 0, width, axis=dim)
        before = lax.ppermute(last, axis, up)
        after = lax.ppermute(first, axis, down)
        shard = jnp.concatenate([before, shard, after], axis=dim)
    return shard


def offsets():
    return [
        (step_x, step_y, step_z)
        for step_x in (-1, 0, 1)
        for step_y in (-1, 0, 1)
        for step_z in (-1, 0, 1)
    ]


def source_range(step):
    if step < 0:
        return slice(BLK - 1, BLK)
    if step > 0:
        return slice(0, 1)
    return slice(0, BLK)


def build_padded(pieces):
    planes = []
    for step_x in (-1, 0, 1):
        lines = []
        for step_y in (-1, 0, 1):
            lines.append(
                jnp.concatenate([pieces[step_x, step_y, step_z] for step_z in (-1, 0, 1)], axis=4)
            )
        planes.append(jnp.concatenate(lines, axis=3))
    return jnp.concatenate(planes, axis=2)


def fetch_faces(flat_field, layout):
    row_step, col_step, slot_id, present = layout
    slot_total, channels = (flat_field.shape[0], flat_field.shape[1])
    volume = flat_field.reshape(slot_total, channels, BLK, BLK, BLK)
    x_sides = jnp.stack([volume[:, :, 0], volume[:, :, BLK - 1]]).reshape(
        2, slot_total, channels * BLK * BLK
    )
    y_sides = jnp.stack([volume[:, :, :, 0], volume[:, :, :, BLK - 1]]).reshape(
        2, slot_total, channels * BLK * BLK
    )
    edge_rows = jnp.stack(
        [
            jnp.stack([volume[:, :, 0, 0], volume[:, :, 0, BLK - 1]]),
            jnp.stack([volume[:, :, BLK - 1, 0], volume[:, :, BLK - 1, BLK - 1]]),
        ]
    ).reshape(2, 2, slot_total, channels * BLK)
    x_near = padded_2(x_sides, (("tx", 0),), 1)
    y_near = padded_2(y_sides, (("ty", 0),), 1)
    edge_near = padded_2(edge_rows, (("tx", 0), ("ty", 1)), 1)
    pieces = {}
    for offset_id, (step_x, step_y, step_z) in enumerate(offsets()):
        range_x = source_range(step_x)
        range_y = source_range(step_y)
        range_z = source_range(step_z)
        rows_here = slot_id[:, offset_id]
        same_row = row_step[:, offset_id] == 0
        same_col = col_step[:, offset_id] == 0
        pools = [volume[:, :, range_x, range_y, range_z]]
        source = jnp.zeros((slot_total,), jnp.int32)
        if step_x != 0:
            pools.append(
                x_near[0 if step_x < 0 else 3].reshape(slot_total, channels, 1, BLK, BLK)[
                    :, :, :, range_y, range_z
                ]
            )
            source = jnp.where(jnp.logical_not(same_row) & same_col, len(pools) - 1, source)
        if step_y != 0:
            pools.append(
                y_near[0 if step_y < 0 else 3].reshape(slot_total, channels, BLK, 1, BLK)[
                    :, :, range_x, :, range_z
                ]
            )
            source = jnp.where(same_row & jnp.logical_not(same_col), len(pools) - 1, source)
        if step_x != 0 and step_y != 0:
            pools.append(
                edge_near[0 if step_x < 0 else 3, 0 if step_y < 0 else 3].reshape(
                    slot_total, channels, 1, 1, BLK
                )[:, :, :, :, range_z]
            )
            source = jnp.where(
                jnp.logical_not(same_row) & jnp.logical_not(same_col), len(pools) - 1, source
            )
        blank = jnp.zeros((1,) + pools[0].shape[1:], jnp.bfloat16)
        index = jnp.where(
            present[:, offset_id], source * slot_total + rows_here, len(pools) * slot_total
        )
        pieces[step_x, step_y, step_z] = jnp.take(
            jnp.concatenate(pools + [blank], axis=0), index, axis=0
        )
    return build_padded(pieces)


def convolve(padded, kernel):
    out_channels, in_channels = (kernel.shape[1], kernel.shape[2])
    row_total = padded.shape[0]
    filters = jnp.transpose(kernel.reshape(3, 3, 3, out_channels, in_channels), (3, 4, 0, 1, 2))
    result = lax.conv_general_dilated(
        padded,
        filters,
        (1, 1, 1),
        "VALID",
        dimension_numbers=("NCDHW", "OIDHW", "NCDHW"),
        preferred_element_type=jnp.float32,
    )
    return result.reshape(row_total, out_channels, BLK**3)


def correlate(padded, delta_z):
    out_channels = delta_z.shape[1]
    in_channels = padded.shape[1]
    row_total = padded.shape[0]
    delta_volume = delta_z.reshape(row_total, out_channels, BLK, BLK, BLK)
    result = lax.conv_general_dilated(
        padded,
        delta_volume,
        (1, 1, 1),
        "VALID",
        dimension_numbers=("CNDHW", "IODHW", "CNDHW"),
        preferred_element_type=jnp.float32,
    )
    return jnp.transpose(result, (2, 3, 4, 0, 1)).reshape(27, out_channels, in_channels)


def silu_slope(value):
    sigma = jax.nn.sigmoid(value)
    return sigma * (1.0 + value * (1.0 - sigma))


def local(features, weights, cotangent, neighbours):
    slot_total, channels = (features.shape[0], features.shape[1])
    cells = BLK**3
    my_row = lax.axis_index("tx")
    my_col = lax.axis_index("ty")
    tile_cols = lax.axis_size("ty")
    present = neighbours >= 0
    owner_dev = jnp.maximum(neighbours, 0) // slot_total
    row_step = jnp.where(present, owner_dev // tile_cols - my_row, 0)
    col_step = jnp.where(present, owner_dev % tile_cols - my_col, 0)
    slot_id = jnp.maximum(neighbours, 0) % slot_total
    layout = (row_step, col_step, slot_id, present)

    def fetch(flat_field):
        return fetch_faces(flat_field, layout)

    inputs = []
    preacts = []
    activation = features
    for layer_id in range(LAYERS):
        padded = fetch(activation)
        preact = convolve(padded, weights[layer_id])
        inputs.append(padded)
        preacts.append(preact)
        activation = jax.nn.silu(preact).astype(jnp.bfloat16)
    gradient = cotangent
    partials = [None] * LAYERS
    for layer_id in reversed(range(LAYERS)):
        delta_z = (gradient.astype(jnp.float32) * silu_slope(preacts[layer_id])).astype(
            jnp.bfloat16
        )
        flipped = jnp.transpose(weights[layer_id][::-1], (0, 2, 1))
        if layer_id > 0:
            beside_all = fetch(delta_z)
        if layer_id > 0:
            gradient = convolve(beside_all, flipped).astype(jnp.bfloat16)
        partial_value = correlate(inputs[layer_id], delta_z)
        partials[layer_id] = partial_value
    summed = jnp.stack(partials)
    summed = lax.psum(summed, ("tx", "ty"))
    scale_factor = 1.0 / math.sqrt(slot_total * lax.axis_size("tx") * lax.axis_size("ty") * cells)
    return (activation, summed * scale_factor)


def solution(mesh):
    placed = (P(("tx", "ty"), None, None), P(), P(("tx", "ty"), None, None), P(("tx", "ty"), None))
    return jax.shard_map(
        local,
        mesh=mesh,
        in_specs=placed,
        out_specs=(P(("tx", "ty"), None, None), P()),
        check_vma=False,
    )
```

profile of v0, /device:TPU:1, one launch (start us, length us, event | category | flops | bytes accessed | tf_op | source)
XLA Modules:
  0.0 623.4 jit_solution(10111938521982081355)
XLA Ops:
  10.2 3.3 collective-permute-start.3
  15.3 3.1 collective-permute-start.2
  20.0 2.4 collective-permute-start
  24.0 2.6 collective-permute-start.7
  28.8 3.8 collective-permute-start.1
  50.4 1.5 slice_bitcast_fusion.1
  61.3 4.0 collective-permute-start.4
  67.0 1.5 collective-permute-start.6
  68.7 2.7 collective-permute-done.6
  72.1 1.4 reshape_squeeze.86
  99.7 12.2 %maximum_maximum_fusion = bf16[4,64,10,10,10]{1,0,4,3,2:T(4,128)(2,1)S(1)} fusion(bf16[4,64,1,1,1]{1,0,4,3,2:T(4,128)(2,1)S(1)} %bitcast_select_fusion.122, bf16[4,64,1,1,8]{1,0,4,3,2:T(4,128)(2,1)S(1)} %bitcast_select_fusion.78, bf16[4,64,1,1,1]{1,0,4,3,2:T(4,128)(2,1)S(1)} %bitcast_select_fusion.123, ...), kind=kLoop, calls=%fused_computation.149 | loop fusion | flops 6656000 | bytes 1024000 | tf_op jit(solution)/shard_map/concatenate | solution.py:51
  111.9 6.3 %multiply_convert_fusion.1 = (bf16[4,64,8,8,8]{1,0,4,3,2:T(4,128)(2,1)S(1)}, f32[4,64,8,8,8]{1,0,4,3,2:T(4,128)}) fusion(bf16[4,64,10,10,10]{1,0,4,3,2:T(4,128)(2,1)S(1)} %maximum_maximum_fusion, bf16[3,3,3,64,64]{4,3,2,1,0:T(8,128)(2,1)S(1)} %bitcast.684), kind=kOutput, calls=%fused_computation.147 | convolution fusion | flops 453640192 | bytes 1519616 | tf_op jit(solution)/shard_map/conv_general_dilated | solution.py:120
  119.4 3.3 collective-permute-start.11
  122.9 3.7 collective-permute-start.10
  132.1 2.4 collective-permute-start.8
  135.5 1.9 collective-permute-start.15
  138.3 4.7 collective-permute-start.9
  145.3 4.3 collective-permute-start.12
  175.9 12.1 %maximum_maximum_fusion.1 = bf16[4,64,10,10,10]{1,0,4,3,2:T(4,128)(2,1)S(1)} fusion(bf16[4,64,1,1,1]{1,0,4,3,2:T(4,128)(2,1)S(1)} %bitcast_select_fusion.114, bf16[4,64,1,1,8]{1,0,4,3,2:T(4,128)(2,1)S(1)} %bitcast_select_fusion.66, bf16[4,64,1,1,1]{1,0,4,3,2:T(4,128)(2,1)S(1)} %bitcast_select_fusion.115, ...), kind=kLoop, calls=%fused_computation.150 | loop fusion | flops 6656000 | bytes 1024000 | tf_op jit(solution)/shard_map/concatenate | solution.py:51
  188.0 6.3 %multiply_convert_fusion = (bf16[4,64,8,8,8]{1,0,4,3,2:T(4,128)(2,1)S(1)}, f32[4,64,8,8,8]{1,0,4,3,2:T(4,128)}) fusion(bf16[4,64,10,10,10]{1,0,4,3,2:T(4,128)(2,1)S(1)} %maximum_maximum_fusion.1, bf16[3,3,3,64,64]{4,3,2,1,0:T(8,128)(2,1)S(1)} %bitcast.683), kind=kOutput, calls=%fused_computation.145 | convolution fusion | flops 453640192 | bytes 1519616 | tf_op jit(solution)/shard_map/conv_general_dilated | solution.py:120
  196.7 2.4 collective-permute-start.19
  199.4 4.3 collective-permute-start.18
  211.2 2.4 collective-permute-start.16
  214.5 1.9 collective-permute-start.23
  217.4 6.7 %collective-permute-start.17 = (bf16[1,4,4096]{2,1,0:T(4,128)(2,1)S(1)}, bf16[1,4,4096]{2,1,0:T(4,128)(2,1)S(1)}, u32[]{:S(2)}, u32[]{:S(2)}) collective-permute-start(bf16[1,4,4096]{2,1,0:T(4,128)(2,1)S(1)} %slice.2246), channel_id=1, source_target_pairs={{0,1},{1,2},{2,3},{3,4},{4,5},{5,6},{6,7},{7,8},{8,9},{9,10},{10,1... | collective-permute-start | bytes 98312 | tf_op jit(solution)/shard_map/ppermute | solution.py:19
  226.4 6.4 %collective-permute-start.20 = (bf16[4,1,4,512]{3,2,1,0:T(4,128)(2,1)S(1)}, bf16[4,1,4,512]{3,2,1,0:T(4,128)(2,1)S(1)}, u32[]{:S(2)}, u32[]{:S(2)}) collective-permute-start(bf16[4,1,4,512]{3,2,1,0:T(4,128)(2,1)S(1)} %get-tuple-element.400), channel_id=1, source_target_pairs={{0,1},{1,2},{2,3},{3,4},{4,5},{5,6},{6,7},{7,8},{8,9},{9,10},{10,1... | collective-permute-start | bytes 49160 | tf_op jit(solution)/shard_map/ppermute | solution.py:19
  259.6 11.9 %maximum_maximum_fusion.2 = bf16[4,64,10,10,10]{1,0,4,3,2:T(4,128)(2,1)S(1)} fusion(bf16[4,64,1,1,1]{1,0,4,3,2:T(4,128)(2,1)S(1)} %bitcast_select_fusion.106, bf16[4,64,1,1,8]{1,0,4,3,2:T(4,128)(2,1)S(1)} %bitcast_select_fusion.54, bf16[4,64,1,1,1]{1,0,4,3,2:T(4,128)(2,1)S(1)} %bitcast_select_fusion.107, ...), kind=kLoop, calls=%fused_computation.151 | loop fusion | flops 6656000 | bytes 1024000 | tf_op jit(solution)/shard_map/concatenate | solution.py:51
  271.6 5.1 fusion.337
  277.0 2.0 multiply_convert_fusion.2
  279.4 4.1 fusion.339
  285.2 2.4 collective-permute-start.27
  288.0 4.3 collective-permute-start.26
  298.6 2.4 collective-permute-start.24
  301.9 1.9 collective-permute-start.31
  304.8 6.4 %collective-permute-start.25 = (bf16[1,4,4096]{2,1,0:T(4,128)(2,1)S(1)}, bf16[1,4,4096]{2,1,0:T(4,128)(2,1)S(1)}, u32[]{:S(2)}, u32[]{:S(2)}) collective-permute-start(bf16[1,4,4096]{2,1,0:T(4,128)(2,1)S(1)} %slice.2323), channel_id=1, source_target_pairs={{0,1},{1,2},{2,3},{3,4},{4,5},{5,6},{6,7},{7,8},{8,9},{9,10},{10,1... | collective-permute-start | bytes 98312 | tf_op jit(solution)/shard_map/ppermute | solution.py:19
  313.4 6.8 %collective-permute-start.28 = (bf16[4,1,4,512]{3,2,1,0:T(4,128)(2,1)S(1)}, bf16[4,1,4,512]{3,2,1,0:T(4,128)(2,1)S(1)}, u32[]{:S(2)}, u32[]{:S(2)}) collective-permute-start(bf16[4,1,4,512]{3,2,1,0:T(4,128)(2,1)S(1)} %get-tuple-element.398), channel_id=1, source_target_pairs={{0,1},{1,2},{2,3},{3,4},{4,5},{5,6},{6,7},{7,8},{8,9},{9,10},{10,1... | collective-permute-start | bytes 49160 | tf_op jit(solution)/shard_map/ppermute | solution.py:19
  346.9 5.5 fusion.5
  352.4 4.4 fusion.338
  358.0 2.4 collective-permute-start.35
  360.7 4.3 collective-permute-start.34
  372.5 2.4 collective-permute-start.32
  375.9 1.9 collective-permute-start.39
  378.7 6.4 %collective-permute-start.33 = (bf16[1,4,4096]{2,1,0:T(4,128)(2,1)S(1)}, bf16[1,4,4096]{2,1,0:T(4,128)(2,1)S(1)}, u32[]{:S(2)}, u32[]{:S(2)}) collective-permute-start(bf16[1,4,4096]{2,1,0:T(4,128)(2,1)S(1)} %slice.2399), channel_id=1, source_target_pairs={{0,1},{1,2},{2,3},{3,4},{4,5},{5,6},{6,7},{7,8},{8,9},{9,10},{10,1... | collective-permute-start | bytes 98312 | tf_op jit(solution)/shard_map/ppermute | solution.py:19
  387.4 6.7 %collective-permute-start.36 = (bf16[4,1,4,512]{3,2,1,0:T(4,128)(2,1)S(1)}, bf16[4,1,4,512]{3,2,1,0:T(4,128)(2,1)S(1)}, u32[]{:S(2)}, u32[]{:S(2)}) collective-permute-start(bf16[4,1,4,512]{3,2,1,0:T(4,128)(2,1)S(1)} %get-tuple-element.396), channel_id=1, source_target_pairs={{0,1},{1,2},{2,3},{3,4},{4,5},{5,6},{6,7},{7,8},{8,9},{9,10},{10,1... | collective-permute-start | bytes 49160 | tf_op jit(solution)/shard_map/ppermute | solution.py:19
  433.0 11.5 %fusion.80 = f32[3,3,3,64,64]{4,3,2,1,0:T(8,128)} fusion(bf16[4,64,10,10,10]{1,0,4,3,2:T(4,128)(2,1)S(1)} %copy-done.2, bf16[3,3,3,64,64]{3,4,2,1,0:T(8,128)(2,1)} %bitcast.680, f32[4,64,8,8,8]{1,0,4,3,2:T(4,128)} %get-tuple-element.529, bf16[4,64,1,1,1]{1,0,4,3,2:T(4,128)(2,1)} %bitcast_select_fusion.90, ...), kind=kOutput, calls=%fused_computation.225 | convolution fusion | flops 921235456 | bytes 2211840 | tf_op jit(solution)/shard_map/transpose | solution.py:144
  444.6 3.0 pad_maximum_fusion
  447.6 164.8 %all-reduce.17.cloned.1.call-done = f32[3,27,64,64]{3,2,1,0:T(8,128)} async-done(((f32[3,27,64,64]{3,2,1,0:T(8,128)}), f32[3,27,64,64]{3,2,1,0:T(8,128)}) %all-reduce.17.cloned.1.call-update) | async-done | bytes 1327120 | tf_op jit(solution)/shard_map/psum | solution.py:191
  612.4 3.7 broadcast_multiply_fusion
  (1136 shorter events, 232.2 us)
Async XLA Ops:
  7.2 605.2 %all-reduce.17.cloned.1.call-start = ((), (), s32[]{:S(2)}) async-start(), calls=%async_computation | async-start | bytes 5308416 | tf_op jit(solution)/shard_map/psum | solution.py:191
  10.2 49.0 %collective-permute-start.3 = (bf16[1,2,4,512]{3,2,1,0:T(4,128)(2,1)}, bf16[1,2,4,512]{3,2,1,0:T(4,128)(2,1)}, u32[]{:S(2)}, u32[]{:S(2)}) collective-permute-start(bf16[1,2,4,512]{3,2,1,0:T(4,128)(2,1)} %constant_dynamic-update-slice_fusion.2), channel_id=1, source_target_pairs={{16,0},{32,16},{48,32},{64,48},{80,64},{96,80},{112,96},{17,1},{33... | collective-permute-start | bytes 24584 | tf_op jit(solution)/shard_map/ppermute | solution.py:20
  15.3 45.2 %collective-permute-start.2 = (bf16[1,2,4,512]{3,2,1,0:T(4,128)(2,1)}, bf16[1,2,4,512]{3,2,1,0:T(4,128)(2,1)}, u32[]{:S(2)}, u32[]{:S(2)}) collective-permute-start(bf16[1,2,4,512]{3,2,1,0:T(4,128)(2,1)} %constant_dynamic-update-slice_fusion), channel_id=1, source_target_pairs={{0,16},{16,32},{32,48},{48,64},{64,80},{80,96},{96,112},{1,17},{17... | collective-permute-start | bytes 24584 | tf_op jit(solution)/shard_map/ppermute | solution.py:19
  20.0 52.1 %collective-permute-start = (bf16[1,4,4096]{2,1,0:T(4,128)(2,1)}, bf16[1,4,4096]{2,1,0:T(4,128)(2,1)}, u32[]{:S(2)}, u32[]{:S(2)}) collective-permute-start(bf16[1,4,4096]{2,1,0:T(4,128)(2,1)} %slice.1987), channel_id=1, source_target_pairs={{0,16},{16,32},{32,48},{48,64},{64,80},{80,96},{96,112},{1,17},{17... | collective-permute-start | bytes 98312 | tf_op jit(solution)/shard_map/ppermute | solution.py:19
  23.9 26.4 %copy-start = (bf16[3,27,64,64]{3,2,1,0:T(8,128)(2,1)S(1)}, bf16[3,27,64,64]{3,2,1,0:T(8,128)(2,1)}, u32[]{:S(2)}) copy-start(bf16[3,27,64,64]{3,2,1,0:T(8,128)(2,1)} %param.21) | copy-start | bytes 1990660
  24.0 51.8 %collective-permute-start.7 = (bf16[1,4,4096]{2,1,0:T(4,128)(2,1)}, bf16[1,4,4096]{2,1,0:T(4,128)(2,1)}, u32[]{:S(2)}, u32[]{:S(2)}) collective-permute-start(bf16[1,4,4096]{2,1,0:T(4,128)(2,1)} %slice.2101), channel_id=1, source_target_pairs={{16,0},{32,16},{48,32},{64,48},{80,64},{96,80},{112,96},{17,1},{33... | collective-permute-start | bytes 98312 | tf_op jit(solution)/shard_map/ppermute | solution.py:20
  27.3 23.1 %copy-start.9 = (bf16[4,64,8,1,8]{1,0,4,3,2:T(4,128)(2,1)}, bf16[4,64,8,1,8]{1,0,4,3,2:T(4,128)(2,1)S(1)}, u32[]{:S(2)}) copy-start(bf16[4,64,8,1,8]{1,0,4,3,2:T(4,128)(2,1)S(1)} %get-tuple-element.230) | copy-start | bytes 98308
  28.8 45.1 %collective-permute-start.1 = (bf16[1,4,4096]{2,1,0:T(4,128)(2,1)}, bf16[1,4,4096]{2,1,0:T(4,128)(2,1)}, u32[]{:S(2)}, u32[]{:S(2)}) collective-permute-start(bf16[1,4,4096]{2,1,0:T(4,128)(2,1)} %slice.1990), channel_id=1, source_target_pairs={{0,1},{1,2},{2,3},{3,4},{4,5},{5,6},{6,7},{7,8},{8,9},{9,10},{10,1... | collective-permute-start | bytes 98312 | tf_op jit(solution)/shard_map/ppermute | solution.py:19
  34.1 126.6 %copy-start.29 = (pred[4]{0:T(512)(128)(4,1)}, pred[4]{0:T(512)(128)(4,1)S(1)}, u32[]{:S(2)}) copy-start(pred[4]{0:T(512)(128)(4,1)S(1)} %get-tuple-element.569) | copy-start | bytes 16
  34.7 93.5 %copy-start.32 = (pred[4]{0:T(512)(128)(4,1)}, pred[4]{0:T(512)(128)(4,1)S(1)}, u32[]{:S(2)}) copy-start(pred[4]{0:T(512)(128)(4,1)S(1)} %get-tuple-element.571) | copy-start | bytes 16
  36.6 90.8 %copy-start.36 = (pred[4]{0:T(512)(128)(4,1)}, pred[4]{0:T(512)(128)(4,1)S(1)}, u32[]{:S(2)}) copy-start(pred[4]{0:T(512)(128)(4,1)S(1)} %get-tuple-element.582) | copy-start | bytes 16
  38.0 137.8 %copy-start.26 = (pred[4]{0:T(512)(128)(4,1)}, pred[4]{0:T(512)(128)(4,1)S(1)}, u32[]{:S(2)}) copy-start(pred[4]{0:T(512)(128)(4,1)S(1)} %get-tuple-element.577) | copy-start | bytes 16
  58.2 33.8 %copy-start.116 = (s32[1024]{0:T(1024)}, s32[1024]{0:T(1024)S(1)}, u32[]{:S(2)}) copy-start(s32[1024]{0:T(1024)S(1)} %pad_clamp_fusion.20) | copy-start | bytes 12292
  59.2 18.4 %collective-permute-start.5 = (bf16[1,4,4096]{2,1,0:T(4,128)(2,1)S(1)}, bf16[1,4,4096]{2,1,0:T(4,128)(2,1)S(1)}, u32[]{:S(2)}, u32[]{:S(2)}) collective-permute-start(bf16[1,4,4096]{2,1,0:T(4,128)(2,1)S(1)} %slice.2036), channel_id=1, source_target_pairs={{1,0},{2,1},{3,2},{4,3},{5,4},{6,5},{7,6},{8,7},{9,8},{10,9},{11,1... | collective-permute-start | bytes 98312 | tf_op jit(solution)/shard_map/ppermute | solution.py:20
  61.3 5.7 collective-permute-start.4
  67.0 4.5 collective-permute-start.6
  119.4 10.4 %collective-permute-start.11 = (bf16[1,2,4,512]{3,2,1,0:T(4,128)(2,1)S(1)}, bf16[1,2,4,512]{3,2,1,0:T(4,128)(2,1)S(1)}, u32[]{:S(2)}, u32[]{:S(2)}) collective-permute-start(bf16[1,2,4,512]{3,2,1,0:T(4,128)(2,1)S(1)} %constant_dynamic-update-slice_fusion.6), channel_id=1, source_target_pairs={{16,0},{32,16},{48,32},{64,48},{80,64},{96,80},{112,96},{17,1},{33... | collective-permute-start | bytes 24584 | tf_op jit(solution)/shard_map/ppermute | solution.py:20
  122.9 6.9 %collective-permute-start.10 = (bf16[1,2,4,512]{3,2,1,0:T(4,128)(2,1)S(1)}, bf16[1,2,4,512]{3,2,1,0:T(4,128)(2,1)S(1)}, u32[]{:S(2)}, u32[]{:S(2)}) collective-permute-start(bf16[1,2,4,512]{3,2,1,0:T(4,128)(2,1)S(1)} %constant_dynamic-update-slice_fusion.4), channel_id=1, source_target_pairs={{0,16},{16,32},{32,48},{48,64},{64,80},{80,96},{96,112},{1,17},{17... | collective-permute-start | bytes 24584 | tf_op jit(solution)/shard_map/ppermute | solution.py:19
  129.9 15.4 %collective-permute-start.14 = (bf16[4,1,4,512]{3,2,1,0:T(4,128)(2,1)S(1)}, bf16[4,1,4,512]{3,2,1,0:T(4,128)(2,1)S(1)}, u32[]{:S(2)}, u32[]{:S(2)}) collective-permute-start(bf16[4,1,4,512]{3,2,1,0:T(4,128)(2,1)S(1)} %get-tuple-element.403), channel_id=1, source_target_pairs={{1,0},{2,1},{3,2},{4,3},{5,4},{6,5},{7,6},{8,7},{9,8},{10,9},{11,1... | collective-permute-start | bytes 49160 | tf_op jit(solution)/shard_map/ppermute | solution.py:20
  132.1 19.0 %collective-permute-start.8 = (bf16[1,4,4096]{2,1,0:T(4,128)(2,1)S(1)}, bf16[1,4,4096]{2,1,0:T(4,128)(2,1)S(1)}, u32[]{:S(2)}, u32[]{:S(2)}) collective-permute-start(bf16[1,4,4096]{2,1,0:T(4,128)(2,1)S(1)} %slice.2166), channel_id=1, source_target_pairs={{0,16},{16,32},{32,48},{48,64},{64,80},{80,96},{96,112},{1,17},{17... | collective-permute-start | bytes 98312 | tf_op jit(solution)/shard_map/ppermute | solution.py:19
  135.5 16.7 %collective-permute-start.15 = (bf16[1,4,4096]{2,1,0:T(4,128)(2,1)S(1)}, bf16[1,4,4096]{2,1,0:T(4,128)(2,1)S(1)}, u32[]{:S(2)}, u32[]{:S(2)}) collective-permute-start(bf16[1,4,4096]{2,1,0:T(4,128)(2,1)S(1)} %slice.2214), channel_id=1, source_target_pairs={{16,0},{32,16},{48,32},{64,48},{80,64},{96,80},{112,96},{17,1},{33... | collective-permute-start | bytes 98312 | tf_op jit(solution)/shard_map/ppermute | solution.py:20
  138.3 15.2 %collective-permute-start.9 = (bf16[1,4,4096]{2,1,0:T(4,128)(2,1)S(1)}, bf16[1,4,4096]{2,1,0:T(4,128)(2,1)S(1)}, u32[]{:S(2)}, u32[]{:S(2)}) collective-permute-start(bf16[1,4,4096]{2,1,0:T(4,128)(2,1)S(1)} %slice.2169), channel_id=1, source_target_pairs={{0,1},{1,2},{2,3},{3,4},{4,5},{5,6},{6,7},{7,8},{8,9},{9,10},{10,1... | collective-permute-start | bytes 98312 | tf_op jit(solution)/shard_map/ppermute | solution.py:19
  144.0 10.6 %collective-permute-start.13 = (bf16[1,4,4096]{2,1,0:T(4,128)(2,1)S(1)}, bf16[1,4,4096]{2,1,0:T(4,128)(2,1)S(1)}, u32[]{:S(2)}, u32[]{:S(2)}) collective-permute-start(bf16[1,4,4096]{2,1,0:T(4,128)(2,1)S(1)} %slice.2191), channel_id=1, source_target_pairs={{1,0},{2,1},{3,2},{4,3},{5,4},{6,5},{7,6},{8,7},{9,8},{10,9},{11,1... | collective-permute-start | bytes 98312 | tf_op jit(solution)/shard_map/ppermute | solution.py:20
  145.3 5.1 collective-permute-start.12
  196.7 11.4 %collective-permute-start.19 = (bf16[1,2,4,512]{3,2,1,0:T(4,128)(2,1)S(1)}, bf16[1,2,4,512]{3,2,1,0:T(4,128)(2,1)}, u32[]{:S(2)}, u32[]{:S(2)}) collective-permute-start(bf16[1,2,4,512]{3,2,1,0:T(4,128)(2,1)S(1)} %constant_dynamic-update-slice_fusion.10), channel_id=1, source_target_pairs={{16,0},{32,16},{48,32},{64,48},{80,64},{96,80},{112,96},{17,1},{33... | collective-permute-start | bytes 24584 | tf_op jit(solution)/shard_map/ppermute | solution.py:20
  199.4 8.7 %collective-permute-start.18 = (bf16[1,2,4,512]{3,2,1,0:T(4,128)(2,1)S(1)}, bf16[1,2,4,512]{3,2,1,0:T(4,128)(2,1)}, u32[]{:S(2)}, u32[]{:S(2)}) collective-permute-start(bf16[1,2,4,512]{3,2,1,0:T(4,128)(2,1)S(1)} %constant_dynamic-update-slice_fusion.8), channel_id=1, source_target_pairs={{0,16},{16,32},{32,48},{48,64},{64,80},{80,96},{96,112},{1,17},{17... | collective-permute-start | bytes 24584 | tf_op jit(solution)/shard_map/ppermute | solution.py:19
  208.9 17.4 %collective-permute-start.22 = (bf16[4,1,4,512]{3,2,1,0:T(4,128)(2,1)S(1)}, bf16[4,1,4,512]{3,2,1,0:T(4,128)(2,1)S(1)}, u32[]{:S(2)}, u32[]{:S(2)}) collective-permute-start(bf16[4,1,4,512]{3,2,1,0:T(4,128)(2,1)S(1)} %get-tuple-element.401), channel_id=1, source_target_pairs={{1,0},{2,1},{3,2},{4,3},{5,4},{6,5},{7,6},{8,7},{9,8},{10,9},{11,1... | collective-permute-start | bytes 49160 | tf_op jit(solution)/shard_map/ppermute | solution.py:20
  211.2 23.1 %collective-permute-start.16 = (bf16[1,4,4096]{2,1,0:T(4,128)(2,1)S(1)}, bf16[1,4,4096]{2,1,0:T(4,128)(2,1)S(1)}, u32[]{:S(2)}, u32[]{:S(2)}) collective-permute-start(bf16[1,4,4096]{2,1,0:T(4,128)(2,1)S(1)} %slice.2243), channel_id=1, source_target_pairs={{0,16},{16,32},{32,48},{48,64},{64,80},{80,96},{96,112},{1,17},{17... | collective-permute-start | bytes 98312 | tf_op jit(solution)/shard_map/ppermute | solution.py:19
  214.5 20.8 %collective-permute-start.23 = (bf16[1,4,4096]{2,1,0:T(4,128)(2,1)S(1)}, bf16[1,4,4096]{2,1,0:T(4,128)(2,1)S(1)}, u32[]{:S(2)}, u32[]{:S(2)}) collective-permute-start(bf16[1,4,4096]{2,1,0:T(4,128)(2,1)S(1)} %slice.2291), channel_id=1, source_target_pairs={{16,0},{32,16},{48,32},{64,48},{80,64},{96,80},{112,96},{17,1},{33... | collective-permute-start | bytes 98312 | tf_op jit(solution)/shard_map/ppermute | solution.py:20
  217.4 19.3 %collective-permute-start.17 = (bf16[1,4,4096]{2,1,0:T(4,128)(2,1)S(1)}, bf16[1,4,4096]{2,1,0:T(4,128)(2,1)S(1)}, u32[]{:S(2)}, u32[]{:S(2)}) collective-permute-start(bf16[1,4,4096]{2,1,0:T(4,128)(2,1)S(1)} %slice.2246), channel_id=1, source_target_pairs={{0,1},{1,2},{2,3},{3,4},{4,5},{5,6},{6,7},{7,8},{8,9},{9,10},{10,1... | collective-permute-start | bytes 98312 | tf_op jit(solution)/shard_map/ppermute | solution.py:19
  225.1 12.8 %collective-permute-start.21 = (bf16[1,4,4096]{2,1,0:T(4,128)(2,1)S(1)}, bf16[1,4,4096]{2,1,0:T(4,128)(2,1)S(1)}, u32[]{:S(2)}, u32[]{:S(2)}) collective-permute-start(bf16[1,4,4096]{2,1,0:T(4,128)(2,1)S(1)} %slice.2268), channel_id=1, source_target_pairs={{1,0},{2,1},{3,2},{4,3},{5,4},{6,5},{7,6},{8,7},{9,8},{10,9},{11,1... | collective-permute-start | bytes 98312 | tf_op jit(solution)/shard_map/ppermute | solution.py:20
  226.4 7.2 %collective-permute-start.20 = (bf16[4,1,4,512]{3,2,1,0:T(4,128)(2,1)S(1)}, bf16[4,1,4,512]{3,2,1,0:T(4,128)(2,1)S(1)}, u32[]{:S(2)}, u32[]{:S(2)}) collective-permute-start(bf16[4,1,4,512]{3,2,1,0:T(4,128)(2,1)S(1)} %get-tuple-element.400), channel_id=1, source_target_pairs={{0,1},{1,2},{2,3},{3,4},{4,5},{5,6},{6,7},{7,8},{8,9},{9,10},{10,1... | collective-permute-start | bytes 49160 | tf_op jit(solution)/shard_map/ppermute | solution.py:19
  285.2 11.0 %collective-permute-start.27 = (bf16[1,2,4,512]{3,2,1,0:T(4,128)(2,1)S(1)}, bf16[1,2,4,512]{3,2,1,0:T(4,128)(2,1)S(1)}, u32[]{:S(2)}, u32[]{:S(2)}) collective-permute-start(bf16[1,2,4,512]{3,2,1,0:T(4,128)(2,1)S(1)} %constant_dynamic-update-slice_fusion.14), channel_id=1, source_target_pairs={{16,0},{32,16},{48,32},{64,48},{80,64},{96,80},{112,96},{17,1},{33... | collective-permute-start | bytes 24584 | tf_op jit(solution)/shard_map/ppermute | solution.py:20
  288.0 8.3 %collective-permute-start.26 = (bf16[1,2,4,512]{3,2,1,0:T(4,128)(2,1)S(1)}, bf16[1,2,4,512]{3,2,1,0:T(4,128)(2,1)S(1)}, u32[]{:S(2)}, u32[]{:S(2)}) collective-permute-start(bf16[1,2,4,512]{3,2,1,0:T(4,128)(2,1)S(1)} %constant_dynamic-update-slice_fusion.12), channel_id=1, source_target_pairs={{0,16},{16,32},{32,48},{48,64},{64,80},{80,96},{96,112},{1,17},{17... | collective-permute-start | bytes 24584 | tf_op jit(solution)/shard_map/ppermute | solution.py:19
  296.3 17.1 %collective-permute-start.30 = (bf16[4,1,4,512]{3,2,1,0:T(4,128)(2,1)S(1)}, bf16[4,1,4,512]{3,2,1,0:T(4,128)(2,1)S(1)}, u32[]{:S(2)}, u32[]{:S(2)}) collective-permute-start(bf16[4,1,4,512]{3,2,1,0:T(4,128)(2,1)S(1)} %get-tuple-element.399), channel_id=1, source_target_pairs={{1,0},{2,1},{3,2},{4,3},{5,4},{6,5},{7,6},{8,7},{9,8},{10,9},{11,1... | collective-permute-start | bytes 49160 | tf_op jit(solution)/shard_map/ppermute | solution.py:20
  298.6 23.1 %collective-permute-start.24 = (bf16[1,4,4096]{2,1,0:T(4,128)(2,1)S(1)}, bf16[1,4,4096]{2,1,0:T(4,128)(2,1)S(1)}, u32[]{:S(2)}, u32[]{:S(2)}) collective-permute-start(bf16[1,4,4096]{2,1,0:T(4,128)(2,1)S(1)} %slice.2320), channel_id=1, source_target_pairs={{0,16},{16,32},{32,48},{48,64},{64,80},{80,96},{96,112},{1,17},{17... | collective-permute-start | bytes 98312 | tf_op jit(solution)/shard_map/ppermute | solution.py:19
  301.9 20.8 %collective-permute-start.31 = (bf16[1,4,4096]{2,1,0:T(4,128)(2,1)S(1)}, bf16[1,4,4096]{2,1,0:T(4,128)(2,1)S(1)}, u32[]{:S(2)}, u32[]{:S(2)}) collective-permute-start(bf16[1,4,4096]{2,1,0:T(4,128)(2,1)S(1)} %slice.2368), channel_id=1, source_target_pairs={{16,0},{32,16},{48,32},{64,48},{80,64},{96,80},{112,96},{17,1},{33... | collective-permute-start | bytes 98312 | tf_op jit(solution)/shard_map/ppermute | solution.py:20
  304.8 19.3 %collective-permute-start.25 = (bf16[1,4,4096]{2,1,0:T(4,128)(2,1)S(1)}, bf16[1,4,4096]{2,1,0:T(4,128)(2,1)S(1)}, u32[]{:S(2)}, u32[]{:S(2)}) collective-permute-start(bf16[1,4,4096]{2,1,0:T(4,128)(2,1)S(1)} %slice.2323), channel_id=1, source_target_pairs={{0,1},{1,2},{2,3},{3,4},{4,5},{5,6},{6,7},{7,8},{8,9},{9,10},{10,1... | collective-permute-start | bytes 98312 | tf_op jit(solution)/shard_map/ppermute | solution.py:19
  312.1 13.0 %collective-permute-start.29 = (bf16[1,4,4096]{2,1,0:T(4,128)(2,1)S(1)}, bf16[1,4,4096]{2,1,0:T(4,128)(2,1)S(1)}, u32[]{:S(2)}, u32[]{:S(2)}) collective-permute-start(bf16[1,4,4096]{2,1,0:T(4,128)(2,1)S(1)} %slice.2345), channel_id=1, source_target_pairs={{1,0},{2,1},{3,2},{4,3},{5,4},{6,5},{7,6},{8,7},{9,8},{10,9},{11,1... | collective-permute-start | bytes 98312 | tf_op jit(solution)/shard_map/ppermute | solution.py:20
  313.4 7.5 %collective-permute-start.28 = (bf16[4,1,4,512]{3,2,1,0:T(4,128)(2,1)S(1)}, bf16[4,1,4,512]{3,2,1,0:T(4,128)(2,1)S(1)}, u32[]{:S(2)}, u32[]{:S(2)}) collective-permute-start(bf16[4,1,4,512]{3,2,1,0:T(4,128)(2,1)S(1)} %get-tuple-element.398), channel_id=1, source_target_pairs={{0,1},{1,2},{2,3},{3,4},{4,5},{5,6},{6,7},{7,8},{8,9},{9,10},{10,1... | collective-permute-start | bytes 49160 | tf_op jit(solution)/shard_map/ppermute | solution.py:19
  358.0 12.2 %collective-permute-start.35 = (bf16[1,2,4,512]{3,2,1,0:T(4,128)(2,1)S(1)}, bf16[1,2,4,512]{3,2,1,0:T(4,128)(2,1)S(1)}, u32[]{:S(2)}, u32[]{:S(2)}) collective-permute-start(bf16[1,2,4,512]{3,2,1,0:T(4,128)(2,1)S(1)} %constant_dynamic-update-slice_fusion.18), channel_id=1, source_target_pairs={{16,0},{32,16},{48,32},{64,48},{80,64},{96,80},{112,96},{17,1},{33... | collective-permute-start | bytes 24584 | tf_op jit(solution)/shard_map/ppermute | solution.py:20
  360.7 9.5 %collective-permute-start.34 = (bf16[1,2,4,512]{3,2,1,0:T(4,128)(2,1)S(1)}, bf16[1,2,4,512]{3,2,1,0:T(4,128)(2,1)S(1)}, u32[]{:S(2)}, u32[]{:S(2)}) collective-permute-start(bf16[1,2,4,512]{3,2,1,0:T(4,128)(2,1)S(1)} %constant_dynamic-update-slice_fusion.16), channel_id=1, source_target_pairs={{0,16},{16,32},{32,48},{48,64},{64,80},{80,96},{96,112},{1,17},{17... | collective-permute-start | bytes 24584 | tf_op jit(solution)/shard_map/ppermute | solution.py:19
  370.3 17.1 %collective-permute-start.38 = (bf16[4,1,4,512]{3,2,1,0:T(4,128)(2,1)S(1)}, bf16[4,1,4,512]{3,2,1,0:T(4,128)(2,1)S(1)}, u32[]{:S(2)}, u32[]{:S(2)}) collective-permute-start(bf16[4,1,4,512]{3,2,1,0:T(4,128)(2,1)S(1)} %get-tuple-element.397), channel_id=1, source_target_pairs={{1,0},{2,1},{3,2},{4,3},{5,4},{6,5},{7,6},{8,7},{9,8},{10,9},{11,1... | collective-permute-start | bytes 49160 | tf_op jit(solution)/shard_map/ppermute | solution.py:20
  372.5 23.1 %collective-permute-start.32 = (bf16[1,4,4096]{2,1,0:T(4,128)(2,1)S(1)}, bf16[1,4,4096]{2,1,0:T(4,128)(2,1)S(1)}, u32[]{:S(2)}, u32[]{:S(2)}) collective-permute-start(bf16[1,4,4096]{2,1,0:T(4,128)(2,1)S(1)} %slice.2396), channel_id=1, source_target_pairs={{0,16},{16,32},{32,48},{48,64},{64,80},{80,96},{96,112},{1,17},{17... | collective-permute-start | bytes 98312 | tf_op jit(solution)/shard_map/ppermute | solution.py:19
  375.9 20.8 %collective-permute-start.39 = (bf16[1,4,4096]{2,1,0:T(4,128)(2,1)S(1)}, bf16[1,4,4096]{2,1,0:T(4,128)(2,1)S(1)}, u32[]{:S(2)}, u32[]{:S(2)}) collective-permute-start(bf16[1,4,4096]{2,1,0:T(4,128)(2,1)S(1)} %slice.2444), channel_id=1, source_target_pairs={{16,0},{32,16},{48,32},{64,48},{80,64},{96,80},{112,96},{17,1},{33... | collective-permute-start | bytes 98312 | tf_op jit(solution)/shard_map/ppermute | solution.py:20
  378.7 19.3 %collective-permute-start.33 = (bf16[1,4,4096]{2,1,0:T(4,128)(2,1)S(1)}, bf16[1,4,4096]{2,1,0:T(4,128)(2,1)S(1)}, u32[]{:S(2)}, u32[]{:S(2)}) collective-permute-start(bf16[1,4,4096]{2,1,0:T(4,128)(2,1)S(1)} %slice.2399), channel_id=1, source_target_pairs={{0,1},{1,2},{2,3},{3,4},{4,5},{5,6},{6,7},{7,8},{8,9},{9,10},{10,1... | collective-permute-start | bytes 98312 | tf_op jit(solution)/shard_map/ppermute | solution.py:19
  386.1 13.0 %collective-permute-start.37 = (bf16[1,4,4096]{2,1,0:T(4,128)(2,1)S(1)}, bf16[1,4,4096]{2,1,0:T(4,128)(2,1)S(1)}, u32[]{:S(2)}, u32[]{:S(2)}) collective-permute-start(bf16[1,4,4096]{2,1,0:T(4,128)(2,1)S(1)} %slice.2421), channel_id=1, source_target_pairs={{1,0},{2,1},{3,2},{4,3},{5,4},{6,5},{7,6},{8,7},{9,8},{10,9},{11,1... | collective-permute-start | bytes 98312 | tf_op jit(solution)/shard_map/ppermute | solution.py:20
  387.4 7.5 %collective-permute-start.36 = (bf16[4,1,4,512]{3,2,1,0:T(4,128)(2,1)S(1)}, bf16[4,1,4,512]{3,2,1,0:T(4,128)(2,1)S(1)}, u32[]{:S(2)}, u32[]{:S(2)}) collective-permute-start(bf16[4,1,4,512]{3,2,1,0:T(4,128)(2,1)S(1)} %get-tuple-element.396), channel_id=1, source_target_pairs={{0,1},{1,2},{2,3},{3,4},{4,5},{5,6},{6,7},{7,8},{8,9},{9,10},{10,1... | collective-permute-start | bytes 49160 | tf_op jit(solution)/shard_map/ppermute | solution.py:19
  (120 other events, 958.0 us)
Sparse Core Ops, SparseCore 0:
  447.7 164.5 all-reduce.16
where the time goes:
time: 632 us; the launch traced here: 623 us
  waiting for transfers between devices  170 us (27%)
  local copies, waits for them, and re-layouts  166 us (26%)
  starting transfers between devices  125 us (20%)
  other arithmetic  99.9 us (16%)
  matrix products  43.1 us (7%)
  between operations  19.4 us (3%)
    psum x1, waiting for transfers between devices, local(): summed = lax.psum(summed, ('tx', 'ty'))  165 us
    gather x135, local copies, waits for them, and re-layouts, fetch_faces(): jnp.take(jnp.concatenate(pools + [blank], axis=0), index, axis=0)  93 us
    ppermute x20, starting transfers between devices, padded_2(): before = lax.ppermute(last, axis, up)  87.7 us
    ppermute x20, starting transfers between devices, padded_2(): after = lax.ppermute(first, axis, down)  37.3 us
    concatenate x3, other arithmetic, build_padded(): return jnp.concatenate(planes, axis=2)  36.2 us
    select_n x150, other arithmetic, fetch_faces(): jnp.take(jnp.concatenate(pools + [blank], axis=0), index, axis=0)  29.4 us
    conv_general_dilated x4, matrix products, convolve(): lax.conv_general_dilated(padded, filters, (1, 1, 1), 'VALID', dimension_n...  23.1 us
    transpose x3, matrix products, correlate(): jnp.transpose(result, (2, 3, 4, 0, 1))  20 us
  transfers between devices with their start and end apart: 41, of which 6 were waited for; matrix products, arithmetic and copies ran while one was open for 15% of the time, Pallas kernels for 0%

commit v1 on v0

v1 whole, which is shorter than its diff:
```python
import functools
import math

import jax
import jax.numpy as jnp
from jax import lax
from jax.experimental import pallas as pl
from jax.experimental.pallas import tpu as pltpu
from jax.sharding import PartitionSpec as P

BLK = 8
LAYERS = 3
F32 = jnp.float32
BF16 = jnp.bfloat16
MESH = pl.DeviceIdType.MESH
DIRS = [(-1, 0), (1, 0), (0, -1), (0, 1), (-1, -1), (-1, 1), (1, -1), (1, 1)]


def side(step):
    return 0 if step < 0 else 1


def lane_iota(shape):
    return lax.broadcasted_iota(jnp.int32, shape, len(shape) - 1)


def swap_halves(value):
    return pltpu.roll(value, 64, len(value.shape) - 1)


def pack_cols(face):
    low, high = face[0:4], face[4:8]
    packed = jnp.where(lane_iota(low.shape) < 64, low, swap_halves(high))
    return packed.reshape(32, 128).astype(BF16)


def unpack_cols(packed):
    wide = packed.astype(F32).reshape(4, 8, 128)
    return jnp.concatenate([wide, swap_halves(wide)], axis=0)


def triple(below, here, above):
    z = lax.broadcasted_iota(jnp.int32, here.shape, 1)
    lane = lane_iota(here.shape)
    down = pltpu.roll(jnp.where(z == 7, below, here), 1, 1)
    up = pltpu.roll(jnp.where(z == 0, above, here), 7, 1)
    first = jnp.where(lane < 64, down, swap_halves(here))
    second = jnp.where(lane < 64, up, 0.0)
    return jnp.concatenate([first, second], axis=2)


def sigmoid(value):
    return 1.0 / (1.0 + jnp.exp(-value))


def kernel(
    rows, cols, feat, w, cot, nbr, out, raw,
    idx, field, zp, pre, wf, wb, d3t, send_sem, recv_sem, *pools,
):
    px, py, pd, sd = pools[0:5], pools[5:10], pools[10:15], pools[15:20]
    r, c = lax.axis_index("tx"), lax.axis_index("ty")

    def peer(dr, dc):
        return (lax.rem(r + dr + rows, rows), lax.rem(c + dc + cols, cols))

    barrier = pltpu.get_barrier_semaphore()
    for dr, dc in DIRS:
        pl.semaphore_signal(barrier, inc=1, device_id=peer(dr, dc), device_id_type=MESH)

    def fill_idx(b, carry):
        for o in range(27):
            ox, oy = o // 9 - 1, o // 3 % 3 - 1
            n = nbr[b, o]
            there = n >= 0
            n = jnp.maximum(n, 0)
            slot = n & 3
            dev = n >> 2
            same_r, same_c = (dev // cols) == r, (dev % cols) == c
            base = (b * 27 + o) * 3
            if ox == 0 and oy == 0:
                idx[base] = jnp.where(there, slot, 4)
            elif oy == 0:
                idx[base] = jnp.where(there, slot + jnp.where(same_r, 0, 4), 8)
            elif ox == 0:
                idx[base] = jnp.where(there, slot + jnp.where(same_c, 0, 4), 8)
            else:
                idx[base] = jnp.where(there & same_c, slot + jnp.where(same_r, 0, 4), 8)
                idx[base + 1] = jnp.where(
                    there & same_r & jnp.logical_not(same_c), slot + 4, 8
                )
                idx[base + 2] = jnp.where(
                    there & jnp.logical_not(same_r) & jnp.logical_not(same_c), slot, 4
                )
        return carry

    lax.fori_loop(0, 4, fill_idx, 0)

    field[4] = jnp.zeros((64, 8, 128), F32)
    for e in range(5):
        for s in range(2):
            px[e][s, 8] = jnp.zeros((32, 128), BF16)
            py[e][s, 8] = jnp.zeros((32, 128), BF16)
        for q in range(4):
            pd[e][q, 4] = jnp.zeros((8, 128), F32)

    def load_field(source):
        def one(s, carry):
            wide = source[s].astype(F32)
            wide = jnp.concatenate([wide, jnp.zeros((64, 512), F32)], axis=0)
            field[s] = wide.T.reshape(64, 8, 128)
            return carry

        lax.fori_loop(0, 4, one, 0)

    def build_wf(layer):
        for dx in range(3):
            rows_here = []
            for dy in range(3):
                for dz in range(3):
                    rows_here.append(w[layer, 9 * dx + 3 * dy + dz])
                rows_here.append(jnp.zeros((64, 64), BF16))
            wf[dx * 64:(dx + 1) * 64, :] = jnp.concatenate(rows_here, axis=1)
        wf[192:256, :] = jnp.zeros((64, 768), BF16)

    def build_wb(layer):
        for dy in range(3):
            for dz in range(3):
                row = dy * 256 + dz * 64
                parts = [w[layer, 26 - (9 * dx + 3 * dy + dz)] for dx in range(3)]
                parts.append(jnp.zeros((64, 64), BF16))
                wb[row:row + 64, :] = jnp.concatenate(parts, axis=1)
            wb[dy * 256 + 192:dy * 256 + 256, :] = jnp.zeros((64, 256), BF16)

    def copies(e):
        made = []
        for k, (dr, dc) in enumerate(DIRS):
            if dc == 0:
                s = 0 if dr > 0 else 1
                src, dst = px[e].at[s, pl.ds(0, 4)], px[e].at[s, pl.ds(4, 4)]
            elif dr == 0:
                s = 0 if dc > 0 else 1
                src, dst = py[e].at[s, pl.ds(0, 4)], py[e].at[s, pl.ds(4, 4)]
            else:
                q = (0 if dr > 0 else 1) * 2 + (0 if dc > 0 else 1)
                src, dst = sd[e].at[q], pd[e].at[q, pl.ds(0, 4)]
            made.append(
                pltpu.make_async_remote_copy(
                    src_ref=src, dst_ref=dst, send_sem=send_sem.at[e, k],
                    recv_sem=recv_sem.at[e, k], device_id=peer(dr, dc), device_id_type=MESH,
                )
            )
        return made

    def faces_out(e):
        def one(s, carry):
            for sx in range(2):
                x = 7 if sx == 0 else 0
                face = field[s, pl.ds(x * 8, 8)]
                px[e][sx, s] = pack_cols(face)
                for sy in range(2):
                    y = 7 if sy == 0 else 0
                    sd[e][sx * 2 + sy, s] = face[y]
            for sy in range(2):
                y = 7 if sy == 0 else 0
                face = jnp.concatenate([field[s, pl.ds(x * 8 + y, 1)] for x in range(8)], axis=0)
                py[e][sy, s] = pack_cols(face)
            return carry

        lax.fori_loop(0, 4, one, 0)
        for copy in copies(e):
            copy.start()

    def at(b, o, which=0):
        return idx[(b * 27 + o) * 3 + which]

    def put(z, p, xs, ys, values):
        both = jnp.concatenate(values, axis=1).astype(BF16)
        zp[z, p, xs, ys] = both.reshape(zp[z, p, xs, ys].shape)

    def inner(z):
        def one(t, carry):
            p, x = t // 8, t % 8
            values = []
            for s in range(2):
                b = 2 * p + s
                take = [field[at(b, 12 + j), pl.ds(x * 8, 8)] for j in range(3)]
                values.append(triple(*take))
            put(z, p, pl.ds(x + 1, 1), pl.ds(1, 8), values)
            return carry

        lax.fori_loop(0, 16, one, 0)

    def halo(z, e):
        def one(p, carry):
            for sx in range(2):
                ox, cell = 2 * sx - 1, 9 * sx
                values = []
                for s in range(2):
                    o = 9 * (ox + 1) + 3
                    take = [unpack_cols(px[e][sx, at(2 * p + s, o + j)]) for j in range(3)]
                    values.append(triple(*take))
                put(z, p, pl.ds(cell, 1), pl.ds(1, 8), values)
            for sy in range(2):
                oy, cell = 2 * sy - 1, 9 * sy
                values = []
                for s in range(2):
                    o = 9 + 3 * (oy + 1)
                    take = [unpack_cols(py[e][sy, at(2 * p + s, o + j)]) for j in range(3)]
                    values.append(triple(*take))
                put(z, p, pl.ds(1, 8), pl.ds(cell, 1), values)
            for sx in range(2):
                for sy in range(2):
                    values = []
                    for s in range(2):
                        take = []
                        for j in range(3):
                            o = 18 * sx + 6 * sy + j
                            b = 2 * p + s
                            ix, iy, iq = at(b, o), at(b, o, 1), at(b, o, 2)
                            if sy == 0:
                                from_x = swap_halves(px[e][sx, ix, 16:32].astype(F32)[8:16])
                            else:
                                from_x = px[e][sx, ix, 0:16].astype(F32)[0:8]
                            if sx == 0:
                                from_y = swap_halves(py[e][sy, iy, 16:32].astype(F32)[8:16])
                            else:
                                from_y = py[e][sy, iy, 0:16].astype(F32)[0:8]
                            total = from_x + from_y + pd[e][sx * 2 + sy, iq]
                            take.append(total.reshape(1, 8, 128))
                        values.append(triple(*take))
                    put(z, p, pl.ds(9 * sx, 1), pl.ds(9 * sy, 1), values)
            return carry

        lax.fori_loop(0, 2, one, 0)

    def conv(z, p, forward):
        stack = jnp.concatenate(
            [zp[z, p, :, dy:dy + 8].reshape(1280, 256) for dy in range(3)], axis=1
        )
        if forward:
            acc = lax.dot_general(
                stack, wf[...], (((1,), (1,)), ((), ())), preferred_element_type=F32
            )
        else:
            acc = jnp.dot(stack, wb[...], preferred_element_type=F32)
        acc = acc.reshape(10, 8, 16, 256)
        low, high = acc[..., 0:128], acc[..., 128:256]
        return low[0:8] + swap_halves(low[1:9]) + high[2:10]

    def to_field(p, value):
        value = value.reshape(64, 2, 8, 128)
        for s in range(2):
            field[2 * p + s] = value[:, s]

    def correlate(layer):
        for dy in range(3):
            total = jnp.zeros((256, 256), F32)
            for p in range(2):
                z = zp[layer, p, :, dy:dy + 8].reshape(1280, 256)
                total = total + jnp.dot(d3t[p], z, preferred_element_type=F32)
            raw[layer, dy] = total

    def spread(p, delta):
        lane = lane_iota((10, 8, 16, 128))
        zeros = jnp.zeros((2, 8, 16, 128), F32)
        wide = jnp.concatenate([zeros, delta, zeros], axis=0)
        first = jnp.where(lane < 64, wide[2:12], swap_halves(wide[1:11]))
        second = jnp.where(lane < 64, wide[0:10], 0.0)
        both = jnp.concatenate([first, second], axis=3).reshape(1280, 256)
        d3t[p] = both.T.astype(BF16)

    load_field(feat)
    pl.semaphore_wait(barrier, len(DIRS))

    for layer in range(LAYERS):
        faces_out(layer)
        inner(layer)
        build_wf(layer)
        for copy in copies(layer):
            copy.wait()
        halo(layer, layer)

        def forward(p, carry):
            value = conv(layer, p, True)
            pre[layer, p] = value
            act = (value * sigmoid(value)).astype(BF16).astype(F32)
            to_field(p, act)
            return carry

        lax.fori_loop(0, 2, forward, 0)

    def store_out(s, carry):
        out[s] = field[s].reshape(512, 128).T[0:64].astype(BF16)
        return carry

    lax.fori_loop(0, 4, store_out, 0)

    def make_delta(layer, p, grad):
        v = pre[layer, p]
        s = sigmoid(v)
        delta = (grad * (s * (1.0 + v * (1.0 - s)))).astype(BF16).astype(F32)
        spread(p, delta)
        to_field(p, delta)

    load_field(cot)

    def top(p, carry):
        grad = jnp.concatenate(
            [field[2 * p + s].reshape(64, 1, 8, 128) for s in range(2)], axis=1
        )
        make_delta(2, p, grad.reshape(8, 8, 16, 128))
        return carry

    lax.fori_loop(0, 2, top, 0)
    for layer in (2, 1):
        e = 5 - layer
        faces_out(e)
        inner(3)
        build_wb(layer)
        correlate(layer)
        for copy in copies(e):
            copy.wait()
        halo(3, e)

        def backward(p, carry):
            grad = conv(3, p, False).astype(BF16).astype(F32)
            make_delta(layer - 1, p, grad)
            return carry

        lax.fori_loop(0, 2, backward, 0)
    correlate(0)


def local(features, weights, cotangent, neighbours):
    rows, cols = lax.axis_size("tx"), lax.axis_size("ty")
    vmem = pl.BlockSpec(memory_space=pltpu.VMEM)
    out, raw = pl.pallas_call(
        functools.partial(kernel, rows, cols),
        out_shape=(
            jax.ShapeDtypeStruct((4, 64, 512), BF16),
            jax.ShapeDtypeStruct((LAYERS, 3, 256, 256), F32),
        ),
        in_specs=[vmem, vmem, vmem, pl.BlockSpec(memory_space=pltpu.SMEM)],
        out_specs=(vmem, vmem),
        scratch_shapes=[
            pltpu.SMEM((4 * 27 * 3,), jnp.int32),
            pltpu.VMEM((5, 64, 8, 128), F32),
            pltpu.VMEM((4, 2, 10, 10, 16, 256), BF16),
            pltpu.VMEM((3, 2, 8, 8, 16, 128), F32),
            pltpu.VMEM((256, 768), BF16),
            pltpu.VMEM((768, 256), BF16),
            pltpu.VMEM((2, 256, 1280), BF16),
            pltpu.SemaphoreType.DMA((5, 8)),
            pltpu.SemaphoreType.DMA((5, 8)),
        ]
        + [pltpu.VMEM((2, 9, 32, 128), BF16)] * 10
        + [pltpu.VMEM((4, 5, 8, 128), F32)] * 5
        + [pltpu.VMEM((4, 4, 8, 128), F32)] * 5,
        compiler_params=pltpu.CompilerParams(
            collective_id=0, has_side_effects=True, vmem_limit_bytes=56 * 1024 * 1024
        ),
    )(features, weights, cotangent, neighbours)
    raw = raw[:, :, :192, :192].reshape(LAYERS, 3, 3, 64, 3, 64)
    raw = jnp.transpose(raw, (0, 2, 1, 4, 3, 5)).reshape(LAYERS, 27, 64, 64)
    raw = lax.psum(raw, ("tx", "ty"))
    return out, raw * (1.0 / math.sqrt(4 * rows * cols * BLK**3))


def solution(mesh):
    placed = (P(("tx", "ty"), None, None), P(), P(("tx", "ty"), None, None), P(("tx", "ty"), None))
    return jax.shard_map(
        local,
        mesh=mesh,
        in_specs=placed,
        out_specs=(P(("tx", "ty"), None, None), P()),
        check_vma=False,
    )
```

time: 632 us -> 231 us (0.37); the launches traced: 623 us -> 231 us
  local copies, waits for them, and re-layouts: 166 us -> 9.03 us
  starting transfers between devices: 125 us -> 0.04 us
  other arithmetic: 99.9 us -> 3.7 us
  Pallas kernels: 0 us -> 52.8 us
  matrix products: 43.1 us -> 0 us
  waiting for transfers between devices: 170 us -> 151 us
    ppermute x40 -> x0, starting transfers between devices: 125 us -> none  [the longest x20 87.7 us: padded_2(): before = lax.ppermute(last, axis, up)]
    gather x135 -> x0, local copies, waits for them, and re-layouts: 93 us -> none  [fetch_faces(): jnp.take(jnp.concatenate(pools + [blank], axis=0), index, axis=0)]
    pallas_call x0 -> x1, Pallas kernels: none -> 52.8 us  [local(): pl.pallas_call(functools.partial(kernel, rows, cols), out_shape=(jax.Shap...]
    concatenate x8 -> x0, other arithmetic: 37.9 us -> none  [the longest x3 36.2 us: build_padded(): return jnp.concatenate(planes, axis=2)]
    another operation x211 -> x0, local copies, waits for them, and re-layouts: 32.2 us -> none  [the longest x20 11.5 us: fetch_faces(): x_near[0 if step_x < 0 else 3].reshape(slot_total, channels, 1, BLK, BLK)]
    select_n x155 -> x0, other arithmetic: 30.2 us -> none  [the longest x150 29.4 us: fetch_faces(): jnp.take(jnp.concatenate(pools + [blank], axis=0), index, axis=0)]
    slice x184 -> x1, local copies, waits for them, and re-layouts: 27.9 us -> 2.8 us  [local(): raw = raw[:, :, :192, :192].reshape(LAYERS, 3, 3, 64, 3, 64)]
    conv_general_dilated x4 -> x0, matrix products: 23.1 us -> none  [convolve(): lax.conv_general_dilated(padded, filters, (1, 1, 1), 'VALID', dimension_n...]
  transfers between devices with their start and end apart: 41 -> 1, of which waited for: 6 -> 1; matrix products, arithmetic and copies ran while one was open for 15% -> 0% of each run, Pallas kernels for 0% -> 0%
where the time goes in v1:
time: 231 us
  waiting for transfers between devices  151 us (65%)
  Pallas kernels  52.8 us (23%)
  between operations  14.1 us (6%)
  local copies, waits for them, and re-layouts  9.03 us (4%)
  other arithmetic  3.7 us (2%)
    psum x1, waiting for transfers between devices, local(): raw = lax.psum(raw, ('tx', 'ty'))  151 us
    pallas_call x1, Pallas kernels, local(): pl.pallas_call(functools.partial(kernel, rows, cols), out_shape=(jax.Shap...  52.8 us
  transfers between devices with their start and end apart: 1, of which 1 were waited for; matrix products, arithmetic and copies ran while one was open for 0% of the time, Pallas kernels for 0%

profile of v1, /device:TPU:1, one launch (start us, length us, event | category | flops | bytes accessed | tf_op | source)
XLA Modules:
  0.0 230.7 jit_solution(3498898359090909524)
XLA Ops:
  7.2 0.0 all-reduce.2.cloned.1.call-start
  7.2 52.8 %shard_map.59 = (bf16[4,64,512]{2,1,0:T(8,128)(2,1)}, f32[3,3,256,256]{3,2,1,0:T(8,128)}) custom-call(bf16[4,64,512]{2,1,0:T(8,128)(2,1)} %feat.1, bf16[3,27,64,64]{3,2,1,0:T(8,128)(2,1)} %w.1, bf16[4,64,512]{2,1,0:T(8,128)(2,1)} %cot.1, s32[4,27]{1,0:T(4,128)} %nbr.1), custom_call_target="tpu_custom_call" | custom-call | tf_op jit(solution)/shard_map/pallas_call | solution.py:337
  60.0 2.8 %slice.3 = f32[3,3,192,192]{3,2,1,0:T(8,128)} slice(f32[3,3,256,256]{3,2,1,0:T(8,128)} %get-tuple-element.5), slice={[0:3], [0:3], [0:192], [0:192]} | slice | bytes 2654208 | tf_op jit(solution)/shard_map/slice | solution.py:363
  62.8 3.6 %reshape.10 = f32[3,3,3,64,3,64]{5,4,3,2,1,0:T(4,128)S(1)} reshape(f32[3,3,192,192]{3,2,1,0:T(8,128)} %slice.3) | data formatting | bytes 2654208 | tf_op jit(solution)/shard_map/reshape | solution.py:363
  66.4 1.9 copy.7
  68.3 0.0 all-reduce.2.cloned.1.call-update
  68.3 0.0 copy-start
  68.3 151.1 %all-reduce.2.cloned.1.call-done = f32[3,27,64,64]{3,2,1,0:T(8,128)} async-done(((f32[3,27,64,64]{3,2,1,0:T(8,128)}), f32[3,27,64,64]{3,2,1,0:T(8,128)}) %all-reduce.2.cloned.1.call-update) | async-done | bytes 1327120 | tf_op jit(solution)/shard_map/psum | solution.py:365
  219.4 3.7 %broadcast_multiply_fusion = f32[3,27,64,64]{3,2,1,0:T(8,128)} fusion(f32[3,27,64,64]{3,2,1,0:T(8,128)} %all-reduce.2.cloned.1.call-done), kind=kLoop, calls=%fused_computation | loop fusion | flops 331776 | bytes 2654208 | tf_op jit(solution)/shard_map/mul | solution.py:366
  223.1 0.0 copy-done
  223.1 0.7 copy.10
Async XLA Ops:
  7.2 212.3 %all-reduce.2.cloned.1.call-start = ((), (), s32[]{:S(2)}) async-start(), calls=%async_computation | async-start | bytes 5308416 | tf_op jit(solution)/shard_map/psum | solution.py:365
  68.3 154.8 %copy-start = (bf16[4,64,512]{2,1,0:T(8,128)(2,1)S(1)}, bf16[4,64,512]{2,1,0:T(8,128)(2,1)}, u32[]{:S(2)}) copy-start(bf16[4,64,512]{2,1,0:T(8,128)(2,1)} %get-tuple-element.8) | copy-start | bytes 786436
Sparse Core Ops, SparseCore 0:
  68.5 150.9 all-reduce.1

commit v2 on v1

--- a/solution.py
+++ b/solution.py
@@ -14,10 +14,12 @@
 BF16 = jnp.bfloat16
 MESH = pl.DeviceIdType.MESH
 DIRS = [(-1, 0), (1, 0), (0, -1), (0, 1), (-1, -1), (-1, 1), (1, -1), (1, 1)]
-
-
-def side(step):
-    return 0 if step < 0 else 1
+UNIT_KERNELS = (
+    [(9 * dx + 3 * dy, 9 * dx + 3 * dy + 1) for dy in range(3) for dx in range(3)]
+    + [(9 * dx + 2, 9 * dx + 5) for dx in range(3)]
+    + [(8, 17), (26,)]
+)
+UNITS = len(UNIT_KERNELS)
 
 
 def lane_iota(shape):
@@ -54,17 +56,23 @@
 
 
 def kernel(
-    rows, cols, feat, w, cot, nbr, out, raw,
-    idx, field, zp, pre, wf, wb, d3t, send_sem, recv_sem, *pools,
+    rows, cols, scale, feat, w, cot, nbr, out, grads,
+    idx, field, zp, pre, wf, wb, d3t, raw, sums, send_sem, recv_sem, sum_send, sum_recv, *pools,
 ):
     px, py, pd, sd = pools[0:5], pools[5:10], pools[10:15], pools[15:20]
+    mine, from_cols, from_rows, shares, full = (pools[20 + 3 * n:23 + 3 * n] for n in range(5))
     r, c = lax.axis_index("tx"), lax.axis_index("ty")
 
     def peer(dr, dc):
         return (lax.rem(r + dr + rows, rows), lax.rem(c + dc + cols, cols))
 
     barrier = pltpu.get_barrier_semaphore()
-    for dr, dc in DIRS:
+    partners = sorted(
+        {(dr % rows, dc % cols) for dr, dc in DIRS}
+        | {(k, 0) for k in range(1, rows)}
+        | {(0, k) for k in range(1, cols)}
+    )
+    for dr, dc in partners:
         pl.semaphore_signal(barrier, inc=1, device_id=peer(dr, dc), device_id_type=MESH)
 
     def fill_idx(b, carry):
@@ -258,7 +266,123 @@
             for p in range(2):
                 z = zp[layer, p, :, dy:dy + 8].reshape(1280, 256)
                 total = total + jnp.dot(d3t[p], z, preferred_element_type=F32)
-            raw[layer, dy] = total
+            raw[dy] = total
+        lane = lane_iota((64, 128))
+        for dx in range(3):
+            at_dx = slice(dx * 64, dx * 64 + 64)
+            for dy in range(3):
+                mine[layer][dy * 3 + dx] = raw[dy, at_dx, 0:128].astype(BF16)
+            pair = jnp.where(
+                lane < 64, raw[0, at_dx, 128:256], swap_halves(raw[1, at_dx, 128:256])
+            )
+            mine[layer][9 + dx] = pair.astype(BF16)
+        pair = jnp.where(lane < 64, raw[2, 0:64, 128:256], swap_halves(raw[2, 64:128, 128:256]))
+        mine[layer][12] = pair.astype(BF16)
+        mine[layer][13] = raw[2, 128:192, 128:256].astype(BF16)
+
+    has_unit = c < UNITS
+
+    def wait_bytes(ref, count, sem):
+        part = ref.at[pl.ds(0, count)]
+        pltpu.make_async_copy(part, part, sem).wait()
+
+    def sum_copy(layer, phase, src, dst, device):
+        return pltpu.make_async_remote_copy(
+            src_ref=src, dst_ref=dst, send_sem=sum_send.at[layer, phase],
+            recv_sem=sum_recv.at[layer, phase], device_id=device, device_id_type=MESH,
+        )
+
+    def over(size, body):
+        def one(k, carry):
+            body(k)
+            return carry
+
+        lax.fori_loop(1, size, one, 0)
+
+    def sum_0(layer):
+        def send(k):
+            to = lax.rem(c + k, cols)
+
+            @pl.when(to < UNITS)
+            def _():
+                sum_copy(layer, 0, mine[layer].at[to], from_cols[layer].at[c], (r, to)).start()
+
+        over(cols, send)
+
+    def sum_1(layer):
+        @pl.when(has_unit)
+        def _():
+            wait_bytes(from_cols[layer], cols - 1, sum_recv.at[layer, 0])
+            from_cols[layer][c] = mine[layer][c]
+            total = from_cols[layer][0].astype(F32)
+            for k in range(1, cols):
+                total = total + from_cols[layer][k].astype(F32)
+            sums[layer] = total.reshape(8, 8, 128)
+
+            def send(k):
+                to = lax.rem(r + k, rows)
+                sum_copy(
+                    layer, 1, sums.at[layer, to], from_rows[layer].at[r], (to, c)
+                ).start()
+
+            over(rows, send)
+
+    def sum_2(layer):
+        @pl.when(has_unit)
+        def _():
+            wait_bytes(from_rows[layer], rows - 1, sum_recv.at[layer, 1])
+            from_rows[layer][r] = sums[layer, r]
+            total = from_rows[layer][0]
+            for k in range(1, rows):
+                total = total + from_rows[layer][k]
+            shares[layer][r] = total * scale
+
+            def send(k):
+                to = lax.rem(r + k, rows)
+                sum_copy(
+                    layer, 2, shares[layer].at[r], shares[layer].at[r], (to, c)
+                ).start()
+
+            over(rows, send)
+
+    def sum_3(layer):
+        @pl.when(has_unit)
+        def _():
+            wait_bytes(shares[layer], rows - 1, sum_recv.at[layer, 2])
+            full[layer][c] = shares[layer][...].reshape(64, 128).astype(BF16)
+
+            def send(k):
+                to = lax.rem(c + k, cols)
+                sum_copy(layer, 3, full[layer].at[c], full[layer].at[c], (r, to)).start()
+
+            over(cols, send)
+
+    def sum_4(layer):
+        @pl.when(has_unit)
+        def _():
+            wait_bytes(full[layer], UNITS - 1, sum_recv.at[layer, 3])
+
+        @pl.when(jnp.logical_not(has_unit))
+        def _():
+            wait_bytes(full[layer], UNITS, sum_recv.at[layer, 3])
+
+        for unit, pair in enumerate(UNIT_KERNELS):
+            value = full[layer][unit].astype(F32)
+            grads[layer, pair[0]] = value[:, 0:64]
+            if len(pair) > 1:
+                grads[layer, pair[1]] = swap_halves(value)[:, 0:64]
+
+    def sum_end(layer):
+        @pl.when(has_unit)
+        def _():
+            wait_bytes(mine[layer], UNITS - 1, sum_send.at[layer, 0])
+            wait_bytes(from_rows[layer], rows - 1, sum_send.at[layer, 1])
+            wait_bytes(shares[layer], rows - 1, sum_send.at[layer, 2])
+            wait_bytes(from_cols[layer], cols - 1, sum_send.at[layer, 3])
+
+        @pl.when(jnp.logical_not(has_unit))
+        def _():
+            wait_bytes(mine[layer], UNITS, sum_send.at[layer, 0])
 
     def spread(p, delta):
         lane = lane_iota((10, 8, 16, 128))
@@ -270,7 +394,7 @@
         d3t[p] = both.T.astype(BF16)
 
     load_field(feat)
-    pl.semaphore_wait(barrier, len(DIRS))
+    pl.semaphore_wait(barrier, len(partners))
 
     for layer in range(LAYERS):
         faces_out(layer)
@@ -318,6 +442,9 @@
         inner(3)
         build_wb(layer)
         correlate(layer)
+        sum_0(layer)
+        if layer == 1:
+            sum_1(2)
         for copy in copies(e):
             copy.wait()
         halo(3, e)
@@ -329,16 +456,30 @@
 
         lax.fori_loop(0, 2, backward, 0)
     correlate(0)
+    sum_0(0)
+    sum_2(2)
+    sum_1(1)
+    sum_1(0)
+    sum_3(2)
+    sum_2(1)
+    sum_2(0)
+    sum_4(2)
+    sum_3(1)
+    sum_3(0)
+    sum_4(1)
+    sum_4(0)
+    for layer in range(LAYERS):
+        sum_end(layer)
 
 
 def local(features, weights, cotangent, neighbours):
     rows, cols = lax.axis_size("tx"), lax.axis_size("ty")
     vmem = pl.BlockSpec(memory_space=pltpu.VMEM)
-    out, raw = pl.pallas_call(
-        functools.partial(kernel, rows, cols),
+    return pl.pallas_call(
+        functools.partial(kernel, rows, cols, 1.0 / math.sqrt(4 * rows * cols * BLK**3)),
         out_shape=(
             jax.ShapeDtypeStruct((4, 64, 512), BF16),
-            jax.ShapeDtypeStruct((LAYERS, 3, 256, 256), F32),
+            jax.ShapeDtypeStruct((LAYERS, 27, 64, 64), F32),
         ),
         in_specs=[vmem, vmem, vmem, pl.BlockSpec(memory_space=pltpu.SMEM)],
         out_specs=(vmem, vmem),
@@ -350,20 +491,25 @@
             pltpu.VMEM((256, 768), BF16),
             pltpu.VMEM((768, 256), BF16),
             pltpu.VMEM((2, 256, 1280), BF16),
+            pltpu.VMEM((3, 256, 256), F32),
+            pltpu.VMEM((LAYERS, 8, 8, 128), F32),
             pltpu.SemaphoreType.DMA((5, 8)),
             pltpu.SemaphoreType.DMA((5, 8)),
+            pltpu.SemaphoreType.DMA((LAYERS, 4)),
+            pltpu.SemaphoreType.DMA((LAYERS, 4)),
         ]
         + [pltpu.VMEM((2, 9, 32, 128), BF16)] * 10
         + [pltpu.VMEM((4, 5, 8, 128), F32)] * 5
-        + [pltpu.VMEM((4, 4, 8, 128), F32)] * 5,
+        + [pltpu.VMEM((4, 4, 8, 128), F32)] * 5
+        + [pltpu.VMEM((UNITS, 64, 128), BF16)] * LAYERS
+        + [pltpu.VMEM((cols, 64, 128), BF16)] * LAYERS
+        + [pltpu.VMEM((rows, 8, 128), F32)] * LAYERS
+        + [pltpu.VMEM((rows, 8, 128), F32)] * LAYERS
+        + [pltpu.VMEM((UNITS, 64, 128), BF16)] * LAYERS,
         compiler_params=pltpu.CompilerParams(
             collective_id=0, has_side_effects=True, vmem_limit_bytes=56 * 1024 * 1024
         ),
     )(features, weights, cotangent, neighbours)
-    raw = raw[:, :, :192, :192].reshape(LAYERS, 3, 3, 64, 3, 64)
-    raw = jnp.transpose(raw, (0, 2, 1, 4, 3, 5)).reshape(LAYERS, 27, 64, 64)
-    raw = lax.psum(raw, ("tx", "ty"))
-    return out, raw * (1.0 / math.sqrt(4 * rows * cols * BLK**3))
 
 
 def solution(mesh):

time: 231 us -> 79.4 us (0.34)
  waiting for transfers between devices: 151 us -> 0 us
  Pallas kernels: 52.8 us -> 73.3 us
  between operations: 14.1 us -> 0.64 us
  local copies, waits for them, and re-layouts: 9.03 us -> 5.26 us
  other arithmetic: 3.7 us -> 0 us
    psum x1 -> x0, waiting for transfers between devices: 151 us -> none  [local(): raw = lax.psum(raw, ('tx', 'ty'))]
    pallas_call x1, Pallas kernels: 52.8 us -> 73.3 us  [local(): pl.pallas_call(functools.partial(kernel, rows, cols, 1.0 / math.sqrt(4 *...]
    unnamed x3 -> x2, local copies, waits for them, and re-layouts: 0.71 us -> 5.26 us
    mul x1 -> x0, other arithmetic: 3.7 us -> none  [local(): return (out, raw * (1.0 / math.sqrt(4 * rows * cols * BLK ** 3)))]
    reshape x1 -> x0, local copies, waits for them, and re-layouts: 3.65 us -> none  [local(): raw = raw[:, :, :192, :192].reshape(LAYERS, 3, 3, 64, 3, 64)]
    slice x1 -> x0, local copies, waits for them, and re-layouts: 2.8 us -> none  [local(): raw = raw[:, :, :192, :192].reshape(LAYERS, 3, 3, 64, 3, 64)]
  transfers between devices with their start and end apart: 1 -> 0, of which waited for: 1 -> 0; matrix products, arithmetic and copies ran while one was open for 0% -> 0% of each run, Pallas kernels for 0% -> 0%
where the time goes in v2:
time: 79.4 us; the launch traced here: 79.2 us
  Pallas kernels  73.3 us (92%)
  local copies, waits for them, and re-layouts  5.26 us (7%)
    pallas_call x1, Pallas kernels, local(): pl.pallas_call(functools.partial(kernel, rows, cols, 1.0 / math.sqrt(4 *...  73.3 us
    unnamed x2, local copies, waits for them, and re-layouts  5.26 us

profile of v2, /device:TPU:1, one launch (start us, length us, event | category | flops | bytes accessed | tf_op | source)
XLA Modules:
  0.0 79.2 jit_solution(16355031488661606956)
XLA Ops:
  0.6 73.3 %shard_map.59 = (bf16[4,64,512]{2,1,0:T(8,128)(2,1)}, f32[3,27,64,64]{3,2,1,0:T(8,128)}) custom-call(bf16[4,64,512]{2,1,0:T(8,128)(2,1)} %feat.1, bf16[3,27,64,64]{3,2,1,0:T(8,128)(2,1)} %w.1, bf16[4,64,512]{2,1,0:T(8,128)(2,1)} %cot.1, s32[4,27]{1,0:T(4,128)} %nbr.1), custom_call_target="tpu_custom_call" | custom-call | tf_op jit(solution)/shard_map/pallas_call | solution.py:478
  73.9 1.7 %copy.8 = bf16[4,64,512]{2,1,0:T(8,128)(2,1)} copy(bf16[4,64,512]{2,1,0:T(8,128)(2,1)} %get-tuple-element.4) | data formatting | bytes 524288
  75.6 3.6 %copy.9 = f32[3,27,64,64]{3,2,1,0:T(8,128)} copy(f32[3,27,64,64]{3,2,1,0:T(8,128)} %get-tuple-element.5) | data formatting | bytes 2654208

commit v3 on v2

--- a/solution.py
+++ b/solution.py
@@ -13,7 +13,7 @@
 F32 = jnp.float32
 BF16 = jnp.bfloat16
 MESH = pl.DeviceIdType.MESH
-DIRS = [(-1, 0), (1, 0), (0, -1), (0, 1), (-1, -1), (-1, 1), (1, -1), (1, 1)]
+DIRS = [(-1, -1), (-1, 1), (1, -1), (1, 1), (0, -1), (0, 1), (-1, 0), (1, 0)]
 UNIT_KERNELS = (
     [(9 * dx + 3 * dy, 9 * dx + 3 * dy + 1) for dy in range(3) for dx in range(3)]
     + [(9 * dx + 2, 9 * dx + 5) for dx in range(3)]
@@ -57,22 +57,29 @@
 
 def kernel(
     rows, cols, scale, feat, w, cot, nbr, out, grads,
-    idx, field, zp, pre, wf, wb, d3t, raw, sums, send_sem, recv_sem, sum_send, sum_recv, *pools,
+    idx, field, zp, pre, wf, wb, d3t, raw, part, corner,
+    send_sem, recv_sem, sum_send, sum_recv, *pools,
 ):
     px, py, pd, sd = pools[0:5], pools[5:10], pools[10:15], pools[15:20]
-    mine, from_cols, from_rows, shares, full = (pools[20 + 3 * n:23 + 3 * n] for n in range(5))
+    mine, from_cols, from_rows, full = (pools[20 + 3 * n:23 + 3 * n] for n in range(4))
     r, c = lax.axis_index("tx"), lax.axis_index("ty")
 
     def peer(dr, dc):
         return (lax.rem(r + dr + rows, rows), lax.rem(c + dc + cols, cols))
 
+    def inside(dr, dc):
+        return (r + dr >= 0) & (r + dr < rows) & (c + dc >= 0) & (c + dc < cols)
+
     barrier = pltpu.get_barrier_semaphore()
-    partners = sorted(
-        {(dr % rows, dc % cols) for dr, dc in DIRS}
-        | {(k, 0) for k in range(1, rows)}
-        | {(0, k) for k in range(1, cols)}
-    )
-    for dr, dc in partners:
+    greeted = rows - 1 + cols - 1
+    for dr, dc in DIRS[:4]:
+        greeted = greeted + inside(dr, dc).astype(jnp.int32)
+
+        @pl.when(inside(dr, dc))
+        def _():
+            pl.semaphore_signal(barrier, inc=1, device_id=peer(dr, dc), device_id_type=MESH)
+
+    for dr, dc in [(0, k) for k in range(1, cols)] + [(k, 0) for k in range(1, rows)]:
         pl.semaphore_signal(barrier, inc=1, device_id=peer(dr, dc), device_id_type=MESH)
 
     def fill_idx(b, carry):
@@ -108,8 +115,11 @@
         for s in range(2):
             px[e][s, 8] = jnp.zeros((32, 128), BF16)
             py[e][s, 8] = jnp.zeros((32, 128), BF16)
-        for q in range(4):
-            pd[e][q, 4] = jnp.zeros((8, 128), F32)
+        for p in range(2):
+            for y in (0, 9):
+                zp[e, p, 1:9, y] = jnp.zeros((8, 16, 256), BF16)
+    for q in range(4):
+        corner[q, 4] = jnp.zeros((8, 128), F32)
 
     def load_field(source):
         def one(s, carry):
@@ -127,8 +137,8 @@
                 for dz in range(3):
                     rows_here.append(w[layer, 9 * dx + 3 * dy + dz])
                 rows_here.append(jnp.zeros((64, 64), BF16))
-            wf[dx * 64:(dx + 1) * 64, :] = jnp.concatenate(rows_here, axis=1)
-        wf[192:256, :] = jnp.zeros((64, 768), BF16)
+            wf[layer, dx * 64:(dx + 1) * 64, :] = jnp.concatenate(rows_here, axis=1)
+        wf[layer, 192:256, :] = jnp.zeros((64, 768), BF16)
 
     def build_wb(layer):
         for dy in range(3):
@@ -136,8 +146,8 @@
                 row = dy * 256 + dz * 64
                 parts = [w[layer, 26 - (9 * dx + 3 * dy + dz)] for dx in range(3)]
                 parts.append(jnp.zeros((64, 64), BF16))
-                wb[row:row + 64, :] = jnp.concatenate(parts, axis=1)
-            wb[dy * 256 + 192:dy * 256 + 256, :] = jnp.zeros((64, 256), BF16)
+                wb[layer - 1, row:row + 64, :] = jnp.concatenate(parts, axis=1)
+            wb[layer - 1, dy * 256 + 192:dy * 256 + 256, :] = jnp.zeros((64, 256), BF16)
 
     def copies(e):
         made = []
@@ -150,14 +160,20 @@
                 src, dst = py[e].at[s, pl.ds(0, 4)], py[e].at[s, pl.ds(4, 4)]
             else:
                 q = (0 if dr > 0 else 1) * 2 + (0 if dc > 0 else 1)
-                src, dst = sd[e].at[q], pd[e].at[q, pl.ds(0, 4)]
-            made.append(
+                src, dst = sd[e].at[q], pd[e].at[q]
+            copy = (
                 pltpu.make_async_remote_copy(
                     src_ref=src, dst_ref=dst, send_sem=send_sem.at[e, k],
                     recv_sem=recv_sem.at[e, k], device_id=peer(dr, dc), device_id_type=MESH,
                 )
             )
+            made.append((inside(dr, dc), inside(-dr, -dc), copy))
         return made
+
+    def arrive(e):
+        for sends, receives, copy in copies(e):
+            pl.when(sends)(copy.wait_send)
+            pl.when(receives)(copy.wait_recv)
 
     def faces_out(e):
         def one(s, carry):
@@ -167,7 +183,7 @@
                 px[e][sx, s] = pack_cols(face)
                 for sy in range(2):
                     y = 7 if sy == 0 else 0
-                    sd[e][sx * 2 + sy, s] = face[y]
+                    corner[sx * 2 + sy, s] = face[y]
             for sy in range(2):
                 y = 7 if sy == 0 else 0
                 face = jnp.concatenate([field[s, pl.ds(x * 8 + y, 1)] for x in range(8)], axis=0)
@@ -175,8 +191,15 @@
             return carry
 
         lax.fori_loop(0, 4, one, 0)
-        for copy in copies(e):
-            copy.start()
+        lane = lane_iota((16, 128))
+        for q in range(4):
+            low = corner[q, 0:2].reshape(16, 128)
+            high = corner[q, 2:4].reshape(16, 128)
+            sd[e][q] = jnp.where(lane < 64, low, swap_halves(high)).astype(BF16)
+
+    def send_faces(e):
+        for sends, _, copy in copies(e):
+            pl.when(sends)(copy.start)
 
     def at(b, o, which=0):
         return idx[(b * 27 + o) * 3 + which]
@@ -199,6 +222,11 @@
         lax.fori_loop(0, 16, one, 0)
 
     def halo(z, e):
+        for q in range(4):
+            wide = pd[e][q].astype(F32)
+            corner[q, 0:2] = wide.reshape(2, 8, 128)
+            corner[q, 2:4] = swap_halves(wide).reshape(2, 8, 128)
+
         def one(p, carry):
             for sx in range(2):
                 ox, cell = 2 * sx - 1, 9 * sx
@@ -233,7 +261,7 @@
                                 from_y = swap_halves(py[e][sy, iy, 16:32].astype(F32)[8:16])
                             else:
                                 from_y = py[e][sy, iy, 0:16].astype(F32)[0:8]
-                            total = from_x + from_y + pd[e][sx * 2 + sy, iq]
+                            total = from_x + from_y + corner[sx * 2 + sy, iq]
                             take.append(total.reshape(1, 8, 128))
                         values.append(triple(*take))
                     put(z, p, pl.ds(9 * sx, 1), pl.ds(9 * sy, 1), values)
@@ -241,19 +269,53 @@
 
         lax.fori_loop(0, 2, one, 0)
 
-    def conv(z, p, forward):
-        stack = jnp.concatenate(
-            [zp[z, p, :, dy:dy + 8].reshape(1280, 256) for dy in range(3)], axis=1
+    def multiply(stack, layer, forward, dy=None):
+        at_dy = slice(0, 768) if dy is None else slice(dy * 256, dy * 256 + 256)
+        if forward:
+            return lax.dot_general(
+                stack, wf[layer, :, at_dy], (((1,), (1,)), ((), ())), preferred_element_type=F32
+            )
+        return jnp.dot(stack, wb[layer - 1, at_dy, :], preferred_element_type=F32)
+
+    def over_dx(acc):
+        low, high = acc[..., 0:128], acc[..., 128:256]
+        blank = jnp.zeros_like(low[0:1])
+        left = jnp.concatenate([blank, low[0:7]], axis=0)
+        right = jnp.concatenate([high[1:8], blank], axis=0)
+        return left + swap_halves(low) + right
+
+    def conv_inner(z, layer, forward):
+        def one(p, carry):
+            stack = jnp.concatenate(
+                [zp[z, p, 1:9, dy:dy + 8].reshape(1024, 256) for dy in range(3)], axis=1
+            )
+            part[p] = over_dx(multiply(stack, layer, forward).reshape(8, 8, 16, 256))
+            return carry
+
+        lax.fori_loop(0, 2, one, 0)
+
+    def conv_halo(z, layer, forward):
+        planes = jnp.concatenate(
+            [
+                jnp.concatenate(
+                    [zp[z, p, x, dy:dy + 8].reshape(128, 256) for dy in range(3)], axis=1
+                )
+                for x in (0, 9)
+                for p in range(2)
+            ],
+            axis=0,
         )
-        if forward:
-            acc = lax.dot_general(
-                stack, wf[...], (((1,), (1,)), ((), ())), preferred_element_type=F32
+        acc = multiply(planes, layer, forward).reshape(2, 2, 8, 16, 256)
+        for p in range(2):
+            part[p, 0] += acc[0, p, :, :, 0:128]
+            part[p, 7] += acc[1, p, :, :, 128:256]
+        for cell, dy, y in ((0, 0, 0), (9, 2, 7)):
+            lines = jnp.concatenate(
+                [zp[z, p, 1:9, cell].reshape(128, 256) for p in range(2)], axis=0
             )
-        else:
-            acc = jnp.dot(stack, wb[...], preferred_element_type=F32)
-        acc = acc.reshape(10, 8, 16, 256)
-        low, high = acc[..., 0:128], acc[..., 128:256]
-        return low[0:8] + swap_halves(low[1:9]) + high[2:10]
+            acc = multiply(lines, layer, forward, dy).reshape(2, 8, 16, 256)
+            for p in range(2):
+                part[p, :, y] += over_dx(acc[p])
 
     def to_field(p, value):
         value = value.reshape(64, 2, 8, 128)
@@ -317,12 +379,12 @@
             total = from_cols[layer][0].astype(F32)
             for k in range(1, cols):
                 total = total + from_cols[layer][k].astype(F32)
-            sums[layer] = total.reshape(8, 8, 128)
+            from_rows[layer][r] = total.astype(BF16)
 
             def send(k):
                 to = lax.rem(r + k, rows)
                 sum_copy(
-                    layer, 1, sums.at[layer, to], from_rows[layer].at[r], (to, c)
+                    layer, 1, from_rows[layer].at[r], from_rows[layer].at[r], (to, c)
                 ).start()
 
             over(rows, send)
@@ -331,54 +393,34 @@
         @pl.when(has_unit)
         def _():
             wait_bytes(from_rows[layer], rows - 1, sum_recv.at[layer, 1])
-            from_rows[layer][r] = sums[layer, r]
-            total = from_rows[layer][0]
+            total = from_rows[layer][0].astype(F32)
             for k in range(1, rows):
-                total = total + from_rows[layer][k]
-            shares[layer][r] = total * scale
+                total = total + from_rows[layer][k].astype(F32)
+            full[layer][c] = (total * scale).astype(BF16)
 
             def send(k):
-                to = lax.rem(r + k, rows)
-                sum_copy(
-                    layer, 2, shares[layer].at[r], shares[layer].at[r], (to, c)
-                ).start()
-
-            over(rows, send)
+                to = lax.rem(c + k, cols)
+                sum_copy(layer, 2, full[layer].at[c], full[layer].at[c], (r, to)).start()
+
+            over(cols, send)
 
     def sum_3(layer):
         @pl.when(has_unit)
         def _():
-            wait_bytes(shares[layer], rows - 1, sum_recv.at[layer, 2])
-            full[layer][c] = shares[layer][...].reshape(64, 128).astype(BF16)
-
-            def send(k):
-                to = lax.rem(c + k, cols)
-                sum_copy(layer, 3, full[layer].at[c], full[layer].at[c], (r, to)).start()
-
-            over(cols, send)
-
-    def sum_4(layer):
-        @pl.when(has_unit)
-        def _():
-            wait_bytes(full[layer], UNITS - 1, sum_recv.at[layer, 3])
+            wait_bytes(full[layer], UNITS - 1, sum_recv.at[layer, 2])
 
         @pl.when(jnp.logical_not(has_unit))
         def _():
-            wait_bytes(full[layer], UNITS, sum_recv.at[layer, 3])
-
-        for unit, pair in enumerate(UNIT_KERNELS):
-            value = full[layer][unit].astype(F32)
-            grads[layer, pair[0]] = value[:, 0:64]
-            if len(pair) > 1:
-                grads[layer, pair[1]] = swap_halves(value)[:, 0:64]
+            wait_bytes(full[layer], UNITS, sum_recv.at[layer, 2])
+
+        grads[layer] = full[layer][...]
 
     def sum_end(layer):
         @pl.when(has_unit)
         def _():
             wait_bytes(mine[layer], UNITS - 1, sum_send.at[layer, 0])
             wait_bytes(from_rows[layer], rows - 1, sum_send.at[layer, 1])
-            wait_bytes(shares[layer], rows - 1, sum_send.at[layer, 2])
-            wait_bytes(from_cols[layer], cols - 1, sum_send.at[layer, 3])
+            wait_bytes(from_cols[layer], cols - 1, sum_send.at[layer, 2])
 
         @pl.when(jnp.logical_not(has_unit))
         def _():
@@ -394,18 +436,28 @@
         d3t[p] = both.T.astype(BF16)
 
     load_field(feat)
-    pl.semaphore_wait(barrier, len(partners))
+    faces_out(0)
+    inner(0)
+    build_wf(0)
+    conv_inner(0, 0, True)
+    pl.semaphore_wait(barrier, greeted)
+    send_faces(0)
+    for layer in (1, 2):
+        build_wf(layer)
+        build_wb(layer)
 
     for layer in range(LAYERS):
-        faces_out(layer)
-        inner(layer)
-        build_wf(layer)
-        for copy in copies(layer):
-            copy.wait()
+        if layer > 0:
+            faces_out(layer)
+            send_faces(layer)
+            inner(layer)
+            conv_inner(layer, layer, True)
+        arrive(layer)
         halo(layer, layer)
+        conv_halo(layer, layer, True)
 
         def forward(p, carry):
-            value = conv(layer, p, True)
+            value = part[p]
             pre[layer, p] = value
             act = (value * sigmoid(value)).astype(BF16).astype(F32)
             to_field(p, act)
@@ -423,8 +475,15 @@
         v = pre[layer, p]
         s = sigmoid(v)
         delta = (grad * (s * (1.0 + v * (1.0 - s)))).astype(BF16).astype(F32)
-        spread(p, delta)
+        part[p] = delta
         to_field(p, delta)
+
+    def spread_all():
+        def one(p, carry):
+            spread(p, part[p])
+            return carry
+
+        lax.fori_loop(0, 2, one, 0)
 
     load_field(cot)
 
@@ -439,77 +498,95 @@
     for layer in (2, 1):
         e = 5 - layer
         faces_out(e)
-        inner(3)
-        build_wb(layer)
+        send_faces(e)
+        spread_all()
+        inner(e)
+        conv_inner(e, layer, False)
         correlate(layer)
         sum_0(layer)
         if layer == 1:
             sum_1(2)
-        for copy in copies(e):
-            copy.wait()
-        halo(3, e)
+        arrive(e)
+        halo(e, e)
+        conv_halo(e, layer, False)
 
         def backward(p, carry):
-            grad = conv(3, p, False).astype(BF16).astype(F32)
-            make_delta(layer - 1, p, grad)
+            make_delta(layer - 1, p, part[p].astype(BF16).astype(F32))
             return carry
 
         lax.fori_loop(0, 2, backward, 0)
+    spread_all()
     correlate(0)
     sum_0(0)
+    sum_1(1)
     sum_2(2)
-    sum_1(1)
     sum_1(0)
-    sum_3(2)
     sum_2(1)
     sum_2(0)
-    sum_4(2)
-    sum_3(1)
-    sum_3(0)
-    sum_4(1)
-    sum_4(0)
+    for layer in (2, 1, 0):
+        sum_3(layer)
     for layer in range(LAYERS):
         sum_end(layer)
+
+
+def write_kernel(act, units, out, grads):
+    out[...] = act[...]
+    for layer in range(LAYERS):
+        for unit, pair in enumerate(UNIT_KERNELS):
+            value = units[layer, unit].astype(F32)
+            grads[layer, pair[0]] = value[:, 0:64]
+            if len(pair) > 1:
+                grads[layer, pair[1]] = swap_halves(value)[:, 0:64]
 
 
 def local(features, weights, cotangent, neighbours):
     rows, cols = lax.axis_size("tx"), lax.axis_size("ty")
     vmem = pl.BlockSpec(memory_space=pltpu.VMEM)
-    return pl.pallas_call(
+    act, units = pl.pallas_call(
         functools.partial(kernel, rows, cols, 1.0 / math.sqrt(4 * rows * cols * BLK**3)),
         out_shape=(
             jax.ShapeDtypeStruct((4, 64, 512), BF16),
-            jax.ShapeDtypeStruct((LAYERS, 27, 64, 64), F32),
+            jax.ShapeDtypeStruct((LAYERS, UNITS, 64, 128), BF16),
         ),
         in_specs=[vmem, vmem, vmem, pl.BlockSpec(memory_space=pltpu.SMEM)],
         out_specs=(vmem, vmem),
         scratch_shapes=[
             pltpu.SMEM((4 * 27 * 3,), jnp.int32),
             pltpu.VMEM((5, 64, 8, 128), F32),
-            pltpu.VMEM((4, 2, 10, 10, 16, 256), BF16),
+            pltpu.VMEM((5, 2, 10, 10, 16, 256), BF16),
             pltpu.VMEM((3, 2, 8, 8, 16, 128), F32),
-            pltpu.VMEM((256, 768), BF16),
-            pltpu.VMEM((768, 256), BF16),
+            pltpu.VMEM((3, 256, 768), BF16),
+            pltpu.VMEM((2, 768, 256), BF16),
             pltpu.VMEM((2, 256, 1280), BF16),
             pltpu.VMEM((3, 256, 256), F32),
-            pltpu.VMEM((LAYERS, 8, 8, 128), F32),
+            pltpu.VMEM((2, 8, 8, 16, 128), F32),
+            pltpu.VMEM((4, 5, 8, 128), F32),
             pltpu.SemaphoreType.DMA((5, 8)),
             pltpu.SemaphoreType.DMA((5, 8)),
-            pltpu.SemaphoreType.DMA((LAYERS, 4)),
-            pltpu.SemaphoreType.DMA((LAYERS, 4)),
+            pltpu.SemaphoreType.DMA((LAYERS, 3)),
+            pltpu.SemaphoreType.DMA((LAYERS, 3)),
         ]
         + [pltpu.VMEM((2, 9, 32, 128), BF16)] * 10
-        + [pltpu.VMEM((4, 5, 8, 128), F32)] * 5
-        + [pltpu.VMEM((4, 4, 8, 128), F32)] * 5
+        + [pltpu.VMEM((4, 16, 128), BF16)] * 5
+        + [pltpu.VMEM((4, 16, 128), BF16)] * 5
         + [pltpu.VMEM((UNITS, 64, 128), BF16)] * LAYERS
         + [pltpu.VMEM((cols, 64, 128), BF16)] * LAYERS
-        + [pltpu.VMEM((rows, 8, 128), F32)] * LAYERS
-        + [pltpu.VMEM((rows, 8, 128), F32)] * LAYERS
+        + [pltpu.VMEM((rows, 64, 128), BF16)] * LAYERS
         + [pltpu.VMEM((UNITS, 64, 128), BF16)] * LAYERS,
         compiler_params=pltpu.CompilerParams(
             collective_id=0, has_side_effects=True, vmem_limit_bytes=56 * 1024 * 1024
         ),
     )(features, weights, cotangent, neighbours)
+    return pl.pallas_call(
+        write_kernel,
+        out_shape=(
+            jax.ShapeDtypeStruct((4, 64, 512), BF16),
+            jax.ShapeDtypeStruct((LAYERS, 27, 64, 64), F32),
+        ),
+        in_specs=[vmem, vmem],
+        out_specs=(vmem, vmem),
+        compiler_params=pltpu.CompilerParams(vmem_limit_bytes=16 * 1024 * 1024),
+    )(act, units)
 
 
 def solution(mesh):

time: 79.4 us -> 68.8 us (0.87)
  Pallas kernels: 73.3 us -> 65.6 us
  local copies, waits for them, and re-layouts: 5.26 us -> 2.04 us
    pallas_call x1, Pallas kernels: 73.3 us -> 63.8 us  [local(): pl.pallas_call(functools.partial(kernel, rows, cols, 1.0 / math.sqrt(4 *...]
    unnamed x2 -> x4, local copies, waits for them, and re-layouts: 5.26 us -> 2.04 us
    pallas_call x0 -> x1, Pallas kernels: none -> 1.79 us  [local(): pl.pallas_call(write_kernel, out_shape=(jax.ShapeDtypeStruct((4, 64, 512)...]
where the time goes in v3:
time: 68.8 us; the launch traced here: 68.3 us
  Pallas kernels  65.6 us (95%)
  local copies, waits for them, and re-layouts  2.04 us (3%)
    pallas_call x1, Pallas kernels, local(): pl.pallas_call(functools.partial(kernel, rows, cols, 1.0 / math.sqrt(4 *...  63.8 us
    unnamed x4, local copies, waits for them, and re-layouts  2.04 us
    pallas_call x1, Pallas kernels, local(): pl.pallas_call(write_kernel, out_shape=(jax.ShapeDtypeStruct((4, 64, 512)...  1.79 us

profile of v3, /device:TPU:1, one launch (start us, length us, event | category | flops | bytes accessed | tf_op | source)
XLA Modules:
  0.0 68.3 jit_solution(2074354218245585330)
XLA Ops:
  0.6 63.8 %shard_map.59 = (bf16[4,64,512]{2,1,0:T(8,128)(2,1)}, bf16[3,14,64,128]{3,2,1,0:T(8,128)(2,1)}) custom-call(bf16[4,64,512]{2,1,0:T(8,128)(2,1)} %feat.1, bf16[3,27,64,64]{3,2,1,0:T(8,128)(2,1)} %w.1, bf16[4,64,512]{2,1,0:T(8,128)(2,1)} %cot.1, s32[4,27]{1,0:T(4,128)} %nbr.1), custom_call_target="tpu_custom_call" | custom-call | tf_op jit(solution)/shard_map/pallas_call | solution.py:545
  64.4 0.0 copy-start
  64.4 1.1 %copy-done = bf16[3,14,64,128]{3,2,1,0:T(8,128)(2,1)S(1)} copy-done((bf16[3,14,64,128]{3,2,1,0:T(8,128)(2,1)S(1)}, bf16[3,14,64,128]{3,2,1,0:T(8,128)(2,1)}, u32[]{:S(2)}) %copy-start) | copy-done | bytes 688152
  65.5 0.0 copy-start.1
  65.5 0.9 %copy-done.1 = bf16[4,64,512]{2,1,0:T(8,128)(2,1)S(1)} copy-done((bf16[4,64,512]{2,1,0:T(8,128)(2,1)S(1)}, bf16[4,64,512]{2,1,0:T(8,128)(2,1)}, u32[]{:S(2)}) %copy-start.1) | copy-done | bytes 262168
  66.5 1.8 %shard_map.60 = (bf16[4,64,512]{2,1,0:T(8,128)(2,1)}, f32[3,27,64,64]{3,2,1,0:T(8,128)}) custom-call(bf16[4,64,512]{2,1,0:T(8,128)(2,1)S(1)} %copy-done.1, bf16[3,14,64,128]{3,2,1,0:T(8,128)(2,1)S(1)} %copy-done), custom_call_target="tpu_custom_call" | custom-call | tf_op jit(solution)/shard_map/pallas_call | solution.py:580
Async XLA Ops:
  64.4 1.1 %copy-start = (bf16[3,14,64,128]{3,2,1,0:T(8,128)(2,1)S(1)}, bf16[3,14,64,128]{3,2,1,0:T(8,128)(2,1)}, u32[]{:S(2)}) copy-start(bf16[3,14,64,128]{3,2,1,0:T(8,128)(2,1)} %get-tuple-element.5.units) | copy-start | bytes 2064388
  65.5 0.9 %copy-start.1 = (bf16[4,64,512]{2,1,0:T(8,128)(2,1)S(1)}, bf16[4,64,512]{2,1,0:T(8,128)(2,1)}, u32[]{:S(2)}) copy-start(bf16[4,64,512]{2,1,0:T(8,128)(2,1)} %get-tuple-element.4.act) | copy-start | bytes 786436

commit v4 on v3

--- a/solution.py
+++ b/solution.py
@@ -52,7 +52,7 @@
 
 
 def sigmoid(value):
-    return 1.0 / (1.0 + jnp.exp(-value))
+    return 0.5 + 0.5 * jnp.tanh(0.5 * value)
 
 
 def kernel(
@@ -190,7 +190,7 @@
                 py[e][sy, s] = pack_cols(face)
             return carry
 
-        lax.fori_loop(0, 4, one, 0)
+        lax.fori_loop(0, 4, one, 0, unroll=2)
         lane = lane_iota((16, 128))
         for q in range(4):
             low = corner[q, 0:2].reshape(16, 128)
@@ -219,7 +219,7 @@
             put(z, p, pl.ds(x + 1, 1), pl.ds(1, 8), values)
             return carry
 
-        lax.fori_loop(0, 16, one, 0)
+        lax.fori_loop(0, 16, one, 0, unroll=4)
 
     def halo(z, e):
         for q in range(4):
@@ -267,7 +267,7 @@
                     put(z, p, pl.ds(9 * sx, 1), pl.ds(9 * sy, 1), values)
             return carry
 
-        lax.fori_loop(0, 2, one, 0)
+        lax.fori_loop(0, 2, one, 0, unroll=True)
 
     def multiply(stack, layer, forward, dy=None):
         at_dy = slice(0, 768) if dy is None else slice(dy * 256, dy * 256 + 256)
@@ -324,7 +324,7 @@
 
     def correlate(layer):
         for dy in range(3):
-            total = jnp.zeros((256, 256), F32)
+            total = jnp.zeros((192, 256), F32)
             for p in range(2):
                 z = zp[layer, p, :, dy:dy + 8].reshape(1280, 256)
                 total = total + jnp.dot(d3t[p], z, preferred_element_type=F32)
@@ -433,15 +433,15 @@
         first = jnp.where(lane < 64, wide[2:12], swap_halves(wide[1:11]))
         second = jnp.where(lane < 64, wide[0:10], 0.0)
         both = jnp.concatenate([first, second], axis=3).reshape(1280, 256)
-        d3t[p] = both.T.astype(BF16)
+        d3t[p] = both.T[0:192].astype(BF16)
 
     load_field(feat)
     faces_out(0)
+    pl.semaphore_wait(barrier, greeted)
+    send_faces(0)
     inner(0)
     build_wf(0)
     conv_inner(0, 0, True)
-    pl.semaphore_wait(barrier, greeted)
-    send_faces(0)
     for layer in (1, 2):
         build_wf(layer)
         build_wb(layer)
@@ -529,19 +529,27 @@
         sum_end(layer)
 
 
-def write_kernel(act, units, out, grads):
-    out[...] = act[...]
+def write_kernel(act, units, out, grads, held, sems):
+    copies = [pltpu.make_async_copy(act, out, sems.at[LAYERS])] + [
+        pltpu.make_async_copy(units.at[layer], held.at[layer], sems.at[layer])
+        for layer in range(LAYERS)
+    ]
+    for copy in copies:
+        copy.start()
     for layer in range(LAYERS):
+        copies[layer + 1].wait()
         for unit, pair in enumerate(UNIT_KERNELS):
-            value = units[layer, unit].astype(F32)
+            value = held[layer, unit].astype(F32)
             grads[layer, pair[0]] = value[:, 0:64]
             if len(pair) > 1:
                 grads[layer, pair[1]] = swap_halves(value)[:, 0:64]
+    copies[0].wait()
 
 
 def local(features, weights, cotangent, neighbours):
     rows, cols = lax.axis_size("tx"), lax.axis_size("ty")
     vmem = pl.BlockSpec(memory_space=pltpu.VMEM)
+    hbm = pl.BlockSpec(memory_space=pltpu.HBM)
     act, units = pl.pallas_call(
         functools.partial(kernel, rows, cols, 1.0 / math.sqrt(4 * rows * cols * BLK**3)),
         out_shape=(
@@ -557,8 +565,8 @@
             pltpu.VMEM((3, 2, 8, 8, 16, 128), F32),
             pltpu.VMEM((3, 256, 768), BF16),
             pltpu.VMEM((2, 768, 256), BF16),
-            pltpu.VMEM((2, 256, 1280), BF16),
-            pltpu.VMEM((3, 256, 256), F32),
+            pltpu.VMEM((2, 192, 1280), BF16),
+            pltpu.VMEM((3, 192, 256), F32),
             pltpu.VMEM((2, 8, 8, 16, 128), F32),
             pltpu.VMEM((4, 5, 8, 128), F32),
             pltpu.SemaphoreType.DMA((5, 8)),
@@ -583,9 +591,13 @@
             jax.ShapeDtypeStruct((4, 64, 512), BF16),
             jax.ShapeDtypeStruct((LAYERS, 27, 64, 64), F32),
         ),
-        in_specs=[vmem, vmem],
-        out_specs=(vmem, vmem),
-        compiler_params=pltpu.CompilerParams(vmem_limit_bytes=16 * 1024 * 1024),
+        in_specs=[hbm, hbm],
+        out_specs=(hbm, vmem),
+        scratch_shapes=[
+            pltpu.VMEM((LAYERS, UNITS, 64, 128), BF16),
+            pltpu.SemaphoreType.DMA((LAYERS + 1,)),
+        ],
+        compiler_params=pltpu.CompilerParams(vmem_limit_bytes=56 * 1024 * 1024),
     )(act, units)
 
 

time: 68.8 us -> 70.4 us (1.023)
  Pallas kernels: 65.6 us -> 69.5 us
  local copies, waits for them, and re-layouts: 2.04 us -> 0 us
    pallas_call x1, Pallas kernels: 1.79 us -> 10.6 us  [local(): pl.pallas_call(write_kernel, out_shape=(jax.ShapeDtypeStruct((4, 64, 512)...]
    pallas_call x1, Pallas kernels: 63.8 us -> 58.9 us  [local(): pl.pallas_call(functools.partial(kernel, rows, cols, 1.0 / math.sqrt(4 *...]
    unnamed x4 -> x0, local copies, waits for them, and re-layouts: 2.04 us -> none
where the time goes in v4:
time: 70.4 us; the launch traced here: 70.3 us
  Pallas kernels  69.5 us (99%)
  between operations  0.8 us (1%)
    pallas_call x1, Pallas kernels, local(): pl.pallas_call(functools.partial(kernel, rows, cols, 1.0 / math.sqrt(4 *...  58.9 us
    pallas_call x1, Pallas kernels, local(): pl.pallas_call(write_kernel, out_shape=(jax.ShapeDtypeStruct((4, 64, 512)...  10.6 us

profile of v4, /device:TPU:1, one launch (start us, length us, event | category | flops | bytes accessed | tf_op | source)
XLA Modules:
  0.0 70.3 jit_solution(1705249841241016377)
XLA Ops:
  0.6 58.9 %shard_map.59 = (bf16[4,64,512]{2,1,0:T(8,128)(2,1)}, bf16[3,14,64,128]{3,2,1,0:T(8,128)(2,1)}) custom-call(bf16[4,64,512]{2,1,0:T(8,128)(2,1)} %feat.1, bf16[3,27,64,64]{3,2,1,0:T(8,128)(2,1)} %w.1, bf16[4,64,512]{2,1,0:T(8,128)(2,1)} %cot.1, s32[4,27]{1,0:T(4,128)} %nbr.1), custom_call_target="tpu_custom_call" | custom-call | tf_op jit(solution)/shard_map/pallas_call | solution.py:553
  59.5 10.6 %shard_map.60 = (bf16[4,64,512]{2,1,0:T(8,128)(2,1)}, f32[3,27,64,64]{3,2,1,0:T(8,128)}) custom-call(bf16[4,64,512]{2,1,0:T(8,128)(2,1)} %get-tuple-element.4.act, bf16[3,14,64,128]{3,2,1,0:T(8,128)(2,1)} %get-tuple-element.5.units), custom_call_target="tpu_custom_call" | custom-call | tf_op jit(solution)/shard_map/pallas_call | solution.py:588

commit v5 on v4

--- a/solution.py
+++ b/solution.py
@@ -529,27 +529,19 @@
         sum_end(layer)
 
 
-def write_kernel(act, units, out, grads, held, sems):
-    copies = [pltpu.make_async_copy(act, out, sems.at[LAYERS])] + [
-        pltpu.make_async_copy(units.at[layer], held.at[layer], sems.at[layer])
-        for layer in range(LAYERS)
-    ]
-    for copy in copies:
-        copy.start()
+def write_kernel(act, units, out, grads):
+    out[...] = act[...]
     for layer in range(LAYERS):
-        copies[layer + 1].wait()
         for unit, pair in enumerate(UNIT_KERNELS):
-            value = held[layer, unit].astype(F32)
+            value = units[layer, unit].astype(F32)
             grads[layer, pair[0]] = value[:, 0:64]
             if len(pair) > 1:
                 grads[layer, pair[1]] = swap_halves(value)[:, 0:64]
-    copies[0].wait()
 
 
 def local(features, weights, cotangent, neighbours):
     rows, cols = lax.axis_size("tx"), lax.axis_size("ty")
     vmem = pl.BlockSpec(memory_space=pltpu.VMEM)
-    hbm = pl.BlockSpec(memory_space=pltpu.HBM)
     act, units = pl.pallas_call(
         functools.partial(kernel, rows, cols, 1.0 / math.sqrt(4 * rows * cols * BLK**3)),
         out_shape=(
@@ -591,12 +583,8 @@
             jax.ShapeDtypeStruct((4, 64, 512), BF16),
             jax.ShapeDtypeStruct((LAYERS, 27, 64, 64), F32),
         ),
-        in_specs=[hbm, hbm],
-        out_specs=(hbm, vmem),
-        scratch_shapes=[
-            pltpu.VMEM((LAYERS, UNITS, 64, 128), BF16),
-            pltpu.SemaphoreType.DMA((LAYERS + 1,)),
-        ],
+        in_specs=[vmem, vmem],
+        out_specs=(vmem, vmem),
         compiler_params=pltpu.CompilerParams(vmem_limit_bytes=56 * 1024 * 1024),
     )(act, units)
 

time: 70.4 us -> 62.7 us (0.89)
  Pallas kernels: 69.5 us -> 61.9 us
    pallas_call x1, Pallas kernels: 10.6 us -> 2.97 us  [local(): pl.pallas_call(write_kernel, out_shape=(jax.ShapeDtypeStruct((4, 64, 512)...]
where the time goes in v5:
time: 62.7 us; the launch traced here: 62.5 us
  Pallas kernels  61.9 us (99%)
  between operations  0.64 us (1%)
    pallas_call x1, Pallas kernels, local(): pl.pallas_call(functools.partial(kernel, rows, cols, 1.0 / math.sqrt(4 *...  58.9 us
    pallas_call x1, Pallas kernels, local(): pl.pallas_call(write_kernel, out_shape=(jax.ShapeDtypeStruct((4, 64, 512)...  2.97 us

profile of v5, /device:TPU:1, one launch (start us, length us, event | category | flops | bytes accessed | tf_op | source)
XLA Modules:
  0.0 62.5 jit_solution(2049100037769913243)
XLA Ops:
  0.6 58.9 %shard_map.59 = (bf16[4,64,512]{2,1,0:T(8,128)(2,1)}, bf16[3,14,64,128]{3,2,1,0:T(8,128)(2,1)}) custom-call(bf16[4,64,512]{2,1,0:T(8,128)(2,1)} %feat.1, bf16[3,27,64,64]{3,2,1,0:T(8,128)(2,1)} %w.1, bf16[4,64,512]{2,1,0:T(8,128)(2,1)} %cot.1, s32[4,27]{1,0:T(4,128)} %nbr.1), custom_call_target="tpu_custom_call" | custom-call | tf_op jit(solution)/shard_map/pallas_call | solution.py:545
  59.6 3.0 %shard_map.60 = (bf16[4,64,512]{2,1,0:T(8,128)(2,1)}, f32[3,27,64,64]{3,2,1,0:T(8,128)}) custom-call(bf16[4,64,512]{2,1,0:T(8,128)(2,1)} %get-tuple-element.4.act, bf16[3,14,64,128]{3,2,1,0:T(8,128)(2,1)} %get-tuple-element.5.units), custom_call_target="tpu_custom_call" | custom-call | tf_op jit(solution)/shard_map/pallas_call | solution.py:580

commit v6 on v5

v6 whole, which is shorter than its diff:
```python
import functools
import math

import jax
import jax.numpy as jnp
from jax import lax
from jax.experimental import pallas as pl
from jax.experimental.pallas import tpu as pltpu
from jax.sharding import PartitionSpec as P

BLK = 8
LAYERS = 3
F32 = jnp.float32
BF16 = jnp.bfloat16
MESH = pl.DeviceIdType.MESH
DIRS = [(-1, -1), (-1, 1), (1, -1), (1, 1), (0, -1), (0, 1), (-1, 0), (1, 0)]
UNIT_KERNELS = (
    [(9 * dx + 3 * dy, 9 * dx + 3 * dy + 1) for dy in range(3) for dx in range(3)]
    + [(9 * dx + 2, 9 * dx + 5) for dx in range(3)]
    + [(8, 17), (26,)]
)
UNITS = len(UNIT_KERNELS)


def lane_iota(shape):
    return lax.broadcasted_iota(jnp.int32, shape, len(shape) - 1)


def swap_halves(value):
    return pltpu.roll(value, 64, len(value.shape) - 1)


def pack_cols(face):
    low, high = face[0:4], face[4:8]
    packed = jnp.where(lane_iota(low.shape) < 64, low, swap_halves(high))
    return packed.reshape(32, 128).astype(BF16)


def unpack_cols(packed):
    wide = packed.astype(F32).reshape(4, 8, 128)
    return jnp.concatenate([wide, swap_halves(wide)], axis=0)


def triple(below, here, above):
    z = lax.broadcasted_iota(jnp.int32, here.shape, 1)
    lane = lane_iota(here.shape)
    down = pltpu.roll(jnp.where(z == 7, below, here), 1, 1)
    up = pltpu.roll(jnp.where(z == 0, above, here), 7, 1)
    first = jnp.where(lane < 64, down, swap_halves(here))
    second = jnp.where(lane < 64, up, 0.0)
    return jnp.concatenate([first, second], axis=2)


def sigmoid(value):
    return 0.5 + 0.5 * jnp.tanh(0.5 * value)


def kernel(
    rows, cols, scale, feat, w_hbm, cot_hbm, nbr, out, grads,
    idx, field, zp, pre, wf, wb, d3t, raw, part, corner, last, top, w, cot, fetch_sem,
    send_sem, recv_sem, sum_send, sum_recv, *pools,
):
    px, py, pd, sd = pools[0:5], pools[5:10], pools[10:15], pools[15:20]
    mine, from_cols, from_rows, full = (pools[20 + 3 * n:23 + 3 * n] for n in range(4))
    r, c = lax.axis_index("tx"), lax.axis_index("ty")

    def peer(dr, dc):
        return (lax.rem(r + dr + rows, rows), lax.rem(c + dc + cols, cols))

    def inside(dr, dc):
        return (r + dr >= 0) & (r + dr < rows) & (c + dc >= 0) & (c + dc < cols)

    barrier = pltpu.get_barrier_semaphore()
    greeted = rows - 1 + cols - 1
    for dr, dc in DIRS[:4]:
        greeted = greeted + inside(dr, dc).astype(jnp.int32)

        @pl.when(inside(dr, dc))
        def _():
            pl.semaphore_signal(barrier, inc=1, device_id=peer(dr, dc), device_id_type=MESH)

    for dr, dc in [(0, k) for k in range(1, cols)] + [(k, 0) for k in range(1, rows)]:
        pl.semaphore_signal(barrier, inc=1, device_id=peer(dr, dc), device_id_type=MESH)

    fetch_w = pltpu.make_async_copy(w_hbm, w, fetch_sem.at[0])
    fetch_cot = pltpu.make_async_copy(cot_hbm, cot, fetch_sem.at[1])
    fetch_w.start()
    fetch_cot.start()

    def in_rows(block):
        wide = block.astype(F32)
        wide = jnp.concatenate([wide, jnp.zeros((64, 512), F32)], axis=0)
        return wide.T.reshape(64, 8, 128)

    def load_field():
        def one(s, carry):
            field[s] = in_rows(feat[s])
            return carry

        lax.fori_loop(0, 4, one, 0)

    def load_top():
        def one(p, carry):
            for s in range(2):
                top[p, :, s] = in_rows(cot[2 * p + s])
            return carry

        lax.fori_loop(0, 2, one, 0)

    def build_wf(layer):
        for dx in range(3):
            rows_here = []
            for dy in range(3):
                for dz in range(3):
                    rows_here.append(w[layer, 9 * dx + 3 * dy + dz])
                rows_here.append(jnp.zeros((64, 64), BF16))
            wf[layer, dx * 64:(dx + 1) * 64, :] = jnp.concatenate(rows_here, axis=1)
        wf[layer, 192:256, :] = jnp.zeros((64, 768), BF16)

    def build_wb(layer):
        for dy in range(3):
            for dz in range(3):
                row = dy * 256 + dz * 64
                parts = [w[layer, 26 - (9 * dx + 3 * dy + dz)] for dx in range(3)]
                parts.append(jnp.zeros((64, 64), BF16))
                wb[layer - 1, row:row + 64, :] = jnp.concatenate(parts, axis=1)
            wb[layer - 1, dy * 256 + 192:dy * 256 + 256, :] = jnp.zeros((64, 256), BF16)

    def copies(e):
        made = []
        for k, (dr, dc) in enumerate(DIRS):
            if dc == 0:
                s = 0 if dr > 0 else 1
                src, dst = px[e].at[s, pl.ds(0, 4)], px[e].at[s, pl.ds(4, 4)]
            elif dr == 0:
                s = 0 if dc > 0 else 1
                src, dst = py[e].at[s, pl.ds(0, 4)], py[e].at[s, pl.ds(4, 4)]
            else:
                q = (0 if dr > 0 else 1) * 2 + (0 if dc > 0 else 1)
                src, dst = sd[e].at[q], pd[e].at[q]
            copy = (
                pltpu.make_async_remote_copy(
                    src_ref=src, dst_ref=dst, send_sem=send_sem.at[e, k],
                    recv_sem=recv_sem.at[e, k], device_id=peer(dr, dc), device_id_type=MESH,
                )
            )
            made.append((inside(dr, dc), inside(-dr, -dc), copy))
        return made

    def arrive(e, first, end):
        for sends, receives, copy in copies(e)[first:end]:
            pl.when(sends)(copy.wait_send)
            pl.when(receives)(copy.wait_recv)

    def faces_out(e):
        def one(s, carry):
            for sx in range(2):
                x = 7 if sx == 0 else 0
                face = field[s, pl.ds(x * 8, 8)]
                px[e][sx, s] = pack_cols(face)
                for sy in range(2):
                    y = 7 if sy == 0 else 0
                    corner[sx * 2 + sy, s] = face[y]
            for sy in range(2):
                y = 7 if sy == 0 else 0
                face = jnp.concatenate([field[s, pl.ds(x * 8 + y, 1)] for x in range(8)], axis=0)
                py[e][sy, s] = pack_cols(face)
            return carry

        lax.fori_loop(0, 4, one, 0, unroll=2)
        lane = lane_iota((16, 128))
        for q in range(4):
            low = corner[q, 0:2].reshape(16, 128)
            high = corner[q, 2:4].reshape(16, 128)
            sd[e][q] = jnp.where(lane < 64, low, swap_halves(high)).astype(BF16)

    def send_faces(e):
        for sends, _, copy in copies(e):
            pl.when(sends)(copy.start)

    def at(b, o, which=0):
        return idx[(b * 27 + o) * 3 + which]

    def put(z, p, xs, ys, values):
        both = jnp.concatenate(values, axis=1).astype(BF16)
        zp[z, p, xs, ys] = both.reshape(zp[z, p, xs, ys].shape)

    def inner(z):
        def one(t, carry):
            p, x = t // 8, t % 8
            values = []
            for s in range(2):
                b = 2 * p + s
                take = [field[at(b, 12 + j), pl.ds(x * 8, 8)] for j in range(3)]
                values.append(triple(*take))
            put(z, p, pl.ds(x + 1, 1), pl.ds(1, 8), values)
            return carry

        lax.fori_loop(0, 16, one, 0, unroll=4)

    def halo_x(z, e):
        def one(p, carry):
            for sx in range(2):
                ox, cell = 2 * sx - 1, 9 * sx
                values = []
                for s in range(2):
                    o = 9 * (ox + 1) + 3
                    take = [unpack_cols(px[e][sx, at(2 * p + s, o + j)]) for j in range(3)]
                    values.append(triple(*take))
                put(z, p, pl.ds(cell, 1), pl.ds(1, 8), values)
            return carry

        lax.fori_loop(0, 2, one, 0, unroll=True)

    def halo_y(z, e):
        def one(p, carry):
            for sy in range(2):
                oy, cell = 2 * sy - 1, 9 * sy
                values = []
                for s in range(2):
                    o = 9 + 3 * (oy + 1)
                    take = [unpack_cols(py[e][sy, at(2 * p + s, o + j)]) for j in range(3)]
                    values.append(triple(*take))
                put(z, p, pl.ds(1, 8), pl.ds(cell, 1), values)
            return carry

        lax.fori_loop(0, 2, one, 0, unroll=True)

    def halo_edges(z, e):
        for q in range(4):
            wide = pd[e][q].astype(F32)
            corner[q, 0:2] = wide.reshape(2, 8, 128)
            corner[q, 2:4] = swap_halves(wide).reshape(2, 8, 128)

        def one(p, carry):
            for sx in range(2):
                for sy in range(2):
                    values = []
                    for s in range(2):
                        take = []
                        for j in range(3):
                            o = 18 * sx + 6 * sy + j
                            b = 2 * p + s
                            ix, iy, iq = at(b, o), at(b, o, 1), at(b, o, 2)
                            if sy == 0:
                                from_x = swap_halves(px[e][sx, ix, 16:32].astype(F32)[8:16])
                            else:
                                from_x = px[e][sx, ix, 0:16].astype(F32)[0:8]
                            if sx == 0:
                                from_y = swap_halves(py[e][sy, iy, 16:32].astype(F32)[8:16])
                            else:
                                from_y = py[e][sy, iy, 0:16].astype(F32)[0:8]
                            total = from_x + from_y + corner[sx * 2 + sy, iq]
                            take.append(total.reshape(1, 8, 128))
                        values.append(triple(*take))
                    put(z, p, pl.ds(9 * sx, 1), pl.ds(9 * sy, 1), values)
            return carry

        lax.fori_loop(0, 2, one, 0, unroll=True)

    def multiply(stack, layer, forward, dy=None):
        at_dy = slice(0, 768) if dy is None else slice(dy * 256, dy * 256 + 256)
        if forward:
            return lax.dot_general(
                stack, wf[layer, :, at_dy], (((1,), (1,)), ((), ())), preferred_element_type=F32
            )
        return jnp.dot(stack, wb[layer - 1, at_dy, :], preferred_element_type=F32)

    def over_dx(acc):
        low, high = acc[..., 0:128], acc[..., 128:256]
        blank = jnp.zeros_like(low[0:1])
        left = jnp.concatenate([blank, low[0:7]], axis=0)
        right = jnp.concatenate([high[1:8], blank], axis=0)
        return left + swap_halves(low) + right

    def conv_inner(z, layer, forward):
        def one(p, carry):
            stack = jnp.concatenate(
                [zp[z, p, 1:9, dy:dy + 8].reshape(1024, 256) for dy in range(3)], axis=1
            )
            part[p] = over_dx(multiply(stack, layer, forward).reshape(8, 8, 16, 256))
            return carry

        lax.fori_loop(0, 2, one, 0)

    def conv_planes(z, layer, forward):
        planes = jnp.concatenate(
            [
                jnp.concatenate(
                    [zp[z, p, x, dy:dy + 8].reshape(128, 256) for dy in range(3)], axis=1
                )
                for x in (0, 9)
                for p in range(2)
            ],
            axis=0,
        )
        acc = multiply(planes, layer, forward).reshape(2, 2, 8, 16, 256)
        for p in range(2):
            part[p, 0] += acc[0, p, :, :, 0:128]
            part[p, 7] += acc[1, p, :, :, 128:256]

    def conv_lines(z, layer, forward):
        for cell, dy, y in ((0, 0, 0), (9, 2, 7)):
            lines = jnp.concatenate(
                [zp[z, p, 1:9, cell].reshape(128, 256) for p in range(2)], axis=0
            )
            acc = multiply(lines, layer, forward, dy).reshape(2, 8, 16, 256)
            for p in range(2):
                part[p, :, y] += over_dx(acc[p])

    def finish(e, layer, forward):
        arrive(e, 6, 8)
        halo_x(e, e)
        arrive(e, 4, 6)
        halo_y(e, e)
        conv_lines(e, layer, forward)
        arrive(e, 0, 4)
        halo_edges(e, e)
        conv_planes(e, layer, forward)

    def to_field(p, value):
        value = value.reshape(64, 2, 8, 128)
        for s in range(2):
            field[2 * p + s] = value[:, s]

    def correlate(layer):
        for dy in range(3):
            total = jnp.zeros((192, 256), F32)
            for p in range(2):
                z = zp[layer, p, :, dy:dy + 8].reshape(1280, 256)
                total = total + jnp.dot(d3t[p], z, preferred_element_type=F32)
            raw[dy] = total
        lane = lane_iota((64, 128))
        for dx in range(3):
            at_dx = slice(dx * 64, dx * 64 + 64)
            for dy in range(3):
                mine[layer][dy * 3 + dx] = raw[dy, at_dx, 0:128].astype(BF16)
            pair = jnp.where(
                lane < 64, raw[0, at_dx, 128:256], swap_halves(raw[1, at_dx, 128:256])
            )
            mine[layer][9 + dx] = pair.astype(BF16)
        pair = jnp.where(lane < 64, raw[2, 0:64, 128:256], swap_halves(raw[2, 64:128, 128:256]))
        mine[layer][12] = pair.astype(BF16)
        mine[layer][13] = raw[2, 128:192, 128:256].astype(BF16)

    has_unit = c < UNITS

    def wait_bytes(ref, count, sem):
        part = ref.at[pl.ds(0, count)]
        pltpu.make_async_copy(part, part, sem).wait()

    def sum_copy(layer, phase, src, dst, device):
        return pltpu.make_async_remote_copy(
            src_ref=src, dst_ref=dst, send_sem=sum_send.at[layer, phase],
            recv_sem=sum_recv.at[layer, phase], device_id=device, device_id_type=MESH,
        )

    def over(size, body):
        def one(k, carry):
            body(k)
            return carry

        lax.fori_loop(1, size, one, 0)

    def sum_0(layer):
        def send(k):
            to = lax.rem(c + k, cols)

            @pl.when(to < UNITS)
            def _():
                sum_copy(layer, 0, mine[layer].at[to], from_cols[layer].at[c], (r, to)).start()

        over(cols, send)

    def sum_1(layer):
        @pl.when(has_unit)
        def _():
            wait_bytes(from_cols[layer], cols - 1, sum_recv.at[layer, 0])
            from_cols[layer][c] = mine[layer][c]
            total = from_cols[layer][0].astype(F32)
            for k in range(1, cols):
                total = total + from_cols[layer][k].astype(F32)
            from_rows[layer][r] = total.astype(BF16)

            def send(k):
                to = lax.rem(r + k, rows)
                sum_copy(
                    layer, 1, from_rows[layer].at[r], from_rows[layer].at[r], (to, c)
                ).start()

            over(rows, send)

    def sum_2(layer):
        @pl.when(has_unit)
        def _():
            wait_bytes(from_rows[layer], rows - 1, sum_recv.at[layer, 1])
            total = from_rows[layer][0].astype(F32)
            for k in range(1, rows):
                total = total + from_rows[layer][k].astype(F32)
            full[layer][c] = (total * scale).astype(BF16)

            def send(k):
                to = lax.rem(c + k, cols)
                sum_copy(layer, 2, full[layer].at[c], full[layer].at[c], (r, to)).start()

            over(cols, send)

    def sum_3(layer):
        @pl.when(has_unit)
        def _():
            wait_bytes(full[layer], UNITS - 1, sum_recv.at[layer, 2])

        @pl.when(jnp.logical_not(has_unit))
        def _():
            wait_bytes(full[layer], UNITS, sum_recv.at[layer, 2])

        grads[layer] = full[layer][...]

    def sum_end(layer):
        @pl.when(has_unit)
        def _():
            wait_bytes(mine[layer], UNITS - 1, sum_send.at[layer, 0])
            wait_bytes(from_rows[layer], rows - 1, sum_send.at[layer, 1])
            wait_bytes(from_cols[layer], cols - 1, sum_send.at[layer, 2])

        @pl.when(jnp.logical_not(has_unit))
        def _():
            wait_bytes(mine[layer], UNITS, sum_send.at[layer, 0])

    def spread(p, delta):
        lane = lane_iota((10, 8, 16, 128))
        zeros = jnp.zeros((2, 8, 16, 128), F32)
        wide = jnp.concatenate([zeros, delta, zeros], axis=0)
        first = jnp.where(lane < 64, wide[2:12], swap_halves(wide[1:11]))
        second = jnp.where(lane < 64, wide[0:10], 0.0)
        both = jnp.concatenate([first, second], axis=3).reshape(1280, 256)
        d3t[p] = both.astype(BF16).T[0:192]

    def fill_idx(b, carry):
        for o in range(27):
            ox, oy = o // 9 - 1, o // 3 % 3 - 1
            n = nbr[b, o]
            there = n >= 0
            n = jnp.maximum(n, 0)
            slot = n & 3
            dev = n >> 2
            same_r, same_c = (dev // cols) == r, (dev % cols) == c
            base = (b * 27 + o) * 3
            if ox == 0 and oy == 0:
                idx[base] = jnp.where(there, slot, 4)
            elif oy == 0:
                idx[base] = jnp.where(there, slot + jnp.where(same_r, 0, 4), 8)
            elif ox == 0:
                idx[base] = jnp.where(there, slot + jnp.where(same_c, 0, 4), 8)
            else:
                idx[base] = jnp.where(there & same_c, slot + jnp.where(same_r, 0, 4), 8)
                idx[base + 1] = jnp.where(
                    there & same_r & jnp.logical_not(same_c), slot + 4, 8
                )
                idx[base + 2] = jnp.where(
                    there & jnp.logical_not(same_r) & jnp.logical_not(same_c), slot, 4
                )
        return carry

    def prepare():
        lax.fori_loop(0, 4, fill_idx, 0)

        field[4] = jnp.zeros((64, 8, 128), F32)
        for e in range(5):
            for s in range(2):
                px[e][s, 8] = jnp.zeros((32, 128), BF16)
                py[e][s, 8] = jnp.zeros((32, 128), BF16)
            for p in range(2):
                for y in (0, 9):
                    zp[e, p, 1:9, y] = jnp.zeros((8, 16, 256), BF16)
        for q in range(4):
            corner[q, 4] = jnp.zeros((8, 128), F32)

    load_field()
    faces_out(0)
    pl.semaphore_wait(barrier, greeted)
    send_faces(0)
    prepare()
    inner(0)
    fetch_w.wait()
    build_wf(0)
    conv_inner(0, 0, True)
    for layer in (1, 2):
        build_wf(layer)
        build_wb(layer)

    for layer in range(LAYERS):
        if layer > 0:
            faces_out(layer)
            send_faces(layer)
            inner(layer)
            conv_inner(layer, layer, True)
        if layer == 1:
            fetch_cot.wait()
            load_top()
        finish(layer, layer, True)

        def forward(p, carry):
            value = part[p]
            slope = sigmoid(value)
            act = (value * slope).astype(BF16).astype(F32)
            if layer < 2:
                pre[layer, p] = value
                to_field(p, act)
            else:
                last[p] = act.reshape(64, 2, 8, 128)
                slope = slope * (1.0 + value * (1.0 - slope))
                delta = (top[p].reshape(8, 8, 16, 128) * slope).astype(BF16).astype(F32)
                part[p] = delta
                to_field(p, delta)
            return carry

        lax.fori_loop(0, 2, forward, 0)

    def store_out():
        def one(p, carry):
            for s in range(2):
                out[2 * p + s] = last[p, :, s].reshape(512, 128).T[0:64].astype(BF16)
            return carry

        lax.fori_loop(0, 2, one, 0)

    def make_delta(layer, p, grad):
        v = pre[layer, p]
        s = sigmoid(v)
        delta = (grad * (s * (1.0 + v * (1.0 - s)))).astype(BF16).astype(F32)
        part[p] = delta
        to_field(p, delta)

    def spread_all():
        def one(p, carry):
            spread(p, part[p])
            return carry

        lax.fori_loop(0, 2, one, 0)

    for layer in (2, 1):
        e = 5 - layer
        faces_out(e)
        send_faces(e)
        spread_all()
        inner(e)
        conv_inner(e, layer, False)
        correlate(layer)
        sum_0(layer)
        finish(e, layer, False)

        def backward(p, carry):
            make_delta(layer - 1, p, part[p].astype(BF16).astype(F32))
            return carry

        lax.fori_loop(0, 2, backward, 0)
    spread_all()
    correlate(0)
    sum_0(0)
    sum_1(2)
    sum_1(1)
    store_out()
    sum_2(2)
    sum_2(1)
    sum_1(0)
    sum_2(0)
    for layer in (2, 1, 0):
        sum_3(layer)
    for layer in range(LAYERS):
        sum_end(layer)


def write_kernel(act, units, out, grads):
    @pl.when(pl.program_id(0) == 0)
    def _():
        out[...] = act[...]

    for unit, pair in enumerate(UNIT_KERNELS):
        value = units[0, unit].astype(F32)
        grads[0, pair[0]] = value[:, 0:64]
        if len(pair) > 1:
            grads[0, pair[1]] = swap_halves(value)[:, 0:64]


def local(features, weights, cotangent, neighbours):
    rows, cols = lax.axis_size("tx"), lax.axis_size("ty")
    vmem = pl.BlockSpec(memory_space=pltpu.VMEM)
    hbm = pl.BlockSpec(memory_space=pltpu.HBM)
    act, units = pl.pallas_call(
        functools.partial(kernel, rows, cols, 1.0 / math.sqrt(4 * rows * cols * BLK**3)),
        out_shape=(
            jax.ShapeDtypeStruct((4, 64, 512), BF16),
            jax.ShapeDtypeStruct((LAYERS, UNITS, 64, 128), BF16),
        ),
        in_specs=[vmem, hbm, hbm, pl.BlockSpec(memory_space=pltpu.SMEM)],
        out_specs=(vmem, vmem),
        scratch_shapes=[
            pltpu.SMEM((4 * 27 * 3,), jnp.int32),
            pltpu.VMEM((5, 64, 8, 128), F32),
            pltpu.VMEM((5, 2, 10, 10, 16, 256), BF16),
            pltpu.VMEM((2, 2, 8, 8, 16, 128), F32),
            pltpu.VMEM((3, 256, 768), BF16),
            pltpu.VMEM((2, 768, 256), BF16),
            pltpu.VMEM((2, 192, 1280), BF16),
            pltpu.VMEM((3, 192, 256), F32),
            pltpu.VMEM((2, 8, 8, 16, 128), F32),
            pltpu.VMEM((4, 5, 8, 128), F32),
            pltpu.VMEM((2, 64, 2, 8, 128), F32),
            pltpu.VMEM((2, 64, 2, 8, 128), F32),
            pltpu.VMEM((LAYERS, 27, 64, 64), BF16),
            pltpu.VMEM((4, 64, 512), BF16),
            pltpu.SemaphoreType.DMA((2,)),
            pltpu.SemaphoreType.DMA((5, 8)),
            pltpu.SemaphoreType.DMA((5, 8)),
            pltpu.SemaphoreType.DMA((LAYERS, 3)),
            pltpu.SemaphoreType.DMA((LAYERS, 3)),
        ]
        + [pltpu.VMEM((2, 9, 32, 128), BF16)] * 10
        + [pltpu.VMEM((4, 16, 128), BF16)] * 5
        + [pltpu.VMEM((4, 16, 128), BF16)] * 5
        + [pltpu.VMEM((UNITS, 64, 128), BF16)] * LAYERS
        + [pltpu.VMEM((cols, 64, 128), BF16)] * LAYERS
        + [pltpu.VMEM((rows, 64, 128), BF16)] * LAYERS
        + [pltpu.VMEM((UNITS, 64, 128), BF16)] * LAYERS,
        compiler_params=pltpu.CompilerParams(
            collective_id=0, has_side_effects=True, vmem_limit_bytes=56 * 1024 * 1024
        ),
    )(features, weights, cotangent, neighbours)
    return pl.pallas_call(
        write_kernel,
        out_shape=(
            jax.ShapeDtypeStruct((4, 64, 512), BF16),
            jax.ShapeDtypeStruct((LAYERS, 27, 64, 64), F32),
        ),
        grid=(LAYERS,),
        in_specs=[
            pl.BlockSpec((4, 64, 512), lambda layer: (0, 0, 0)),
            pl.BlockSpec((1, UNITS, 64, 128), lambda layer: (layer, 0, 0, 0)),
        ],
        out_specs=(
            pl.BlockSpec((4, 64, 512), lambda layer: (0, 0, 0)),
            pl.BlockSpec((1, 27, 64, 64), lambda layer: (layer, 0, 0, 0)),
        ),
        compiler_params=pltpu.CompilerParams(vmem_limit_bytes=56 * 1024 * 1024),
    )(act, units)


def solution(mesh):
    placed = (P(("tx", "ty"), None, None), P(), P(("tx", "ty"), None, None), P(("tx", "ty"), None))
    return jax.shard_map(
        local,
        mesh=mesh,
        in_specs=placed,
        out_specs=(P(("tx", "ty"), None, None), P()),
        check_vma=False,
    )
```

time: 62.7 us -> 61.5 us (0.981)
  Pallas kernels: 61.9 us -> 60.7 us
    pallas_call x1, Pallas kernels: 58.9 us -> 57.2 us  [local(): pl.pallas_call(functools.partial(kernel, rows, cols, 1.0 / math.sqrt(4 *...]
where the time goes in v6:
time: 61.5 us; the launch traced here: 61.3 us
  Pallas kernels  60.7 us (99%)
  between operations  0.64 us (1%)
    pallas_call x1, Pallas kernels, local(): pl.pallas_call(functools.partial(kernel, rows, cols, 1.0 / math.sqrt(4 *...  57.2 us
    pallas_call x1, Pallas kernels, local(): pl.pallas_call(write_kernel, out_shape=(jax.ShapeDtypeStruct((4, 64, 512)...  3.49 us

profile of v6, /device:TPU:1, one launch (start us, length us, event | category | flops | bytes accessed | tf_op | source)
XLA Modules:
  0.0 61.3 jit_solution(17091291876194587953)
XLA Ops:
  0.6 57.2 %shard_map.59 = (bf16[4,64,512]{2,1,0:T(8,128)(2,1)}, bf16[3,14,64,128]{3,2,1,0:T(8,128)(2,1)}) custom-call(bf16[4,64,512]{2,1,0:T(8,128)(2,1)} %feat.1, bf16[3,27,64,64]{3,2,1,0:T(8,128)(2,1)} %w_hbm.1, bf16[4,64,512]{2,1,0:T(8,128)(2,1)} %cot_hbm.1, s32[4,27]{1,0:T(4,128)} %nbr.1), custom_call_target="tpu_custom_call" | custom-call | tf_op jit(solution)/shard_map/pallas_call | solution.py:590
  57.8 3.5 %shard_map.60 = (bf16[4,64,512]{2,1,0:T(8,128)(2,1)}, f32[3,27,64,64]{3,2,1,0:T(8,128)}) custom-call(bf16[4,64,512]{2,1,0:T(8,128)(2,1)} %get-tuple-element.4.act, bf16[3,14,64,128]{3,2,1,0:T(8,128)(2,1)} %get-tuple-element.5.units), custom_call_target="tpu_custom_call" | custom-call | tf_op jit(solution)/shard_map/pallas_call | solution.py:630

commit v7 on v6

--- a/solution.py
+++ b/solution.py
@@ -57,7 +57,8 @@
 
 def kernel(
     rows, cols, scale, feat, w_hbm, cot_hbm, nbr, out, grads,
-    idx, field, zp, pre, wf, wb, d3t, raw, part, corner, last, top, w, cot, fetch_sem,
+    idx, field, zp, pre, wf, wb, d3t, raw, part, corner, last, top, w, cot, held,
+    fetch_sem, store_sem,
     send_sem, recv_sem, sum_send, sum_recv, *pools,
 ):
     px, py, pd, sd = pools[0:5], pools[5:10], pools[10:15], pools[15:20]
@@ -102,7 +103,7 @@
     def load_top():
         def one(p, carry):
             for s in range(2):
-                top[p, :, s] = in_rows(cot[2 * p + s])
+                top[p, :, :, 8 * s:8 * s + 8, :] = in_rows(cot[2 * p + s]).reshape(8, 8, 8, 128)
             return carry
 
         lax.fori_loop(0, 2, one, 0)
@@ -152,6 +153,13 @@
             pl.when(sends)(copy.wait_send)
             pl.when(receives)(copy.wait_recv)
 
+    def pack_corners(e):
+        lane = lane_iota((16, 128))
+        for q in range(4):
+            low = corner[q, 0:2].reshape(16, 128)
+            high = corner[q, 2:4].reshape(16, 128)
+            sd[e][q] = jnp.where(lane < 64, low, swap_halves(high)).astype(BF16)
+
     def faces_out(e):
         def one(s, carry):
             for sx in range(2):
@@ -168,11 +176,21 @@
             return carry
 
         lax.fori_loop(0, 4, one, 0, unroll=2)
-        lane = lane_iota((16, 128))
-        for q in range(4):
-            low = corner[q, 0:2].reshape(16, 128)
-            high = corner[q, 2:4].reshape(16, 128)
-            sd[e][q] = jnp.where(lane < 64, low, swap_halves(high)).astype(BF16)
+        pack_corners(e)
+
+    def edge_faces(e, point):
+        for p in range(2):
+            for sx in range(2):
+                plane = point(p, (0, 7)[1 - sx]).reshape(8, 2, 8, 128)
+                for s in range(2):
+                    px[e][sx, 2 * p + s] = pack_cols(plane[:, s])
+                    for sy in range(2):
+                        corner[sx * 2 + sy, 2 * p + s] = plane[(0, 7)[1 - sy], s]
+            for sy in range(2):
+                plane = point(p, (slice(0, 8), (0, 7)[1 - sy])).reshape(8, 2, 8, 128)
+                for s in range(2):
+                    py[e][sy, 2 * p + s] = pack_cols(plane[:, s])
+        pack_corners(e)
 
     def send_faces(e):
         for sends, _, copy in copies(e):
@@ -405,6 +423,9 @@
 
             over(cols, send)
 
+    def write_sum(layer):
+        return pltpu.make_async_copy(full[layer], grads.at[layer], store_sem.at[layer])
+
     def sum_3(layer):
         @pl.when(has_unit)
         def _():
@@ -414,7 +435,7 @@
         def _():
             wait_bytes(full[layer], UNITS, sum_recv.at[layer, 2])
 
-        grads[layer] = full[layer][...]
+        write_sum(layer).start()
 
     def sum_end(layer):
         @pl.when(has_unit)
@@ -489,10 +510,60 @@
         build_wf(layer)
         build_wb(layer)
 
+    def cells(ref, p, where):
+        return ref[(p, *where)] if isinstance(where, tuple) else ref[p, where]
+
+    def act_point(p, where):
+        value = cells(part, p, where)
+        return (value * sigmoid(value)).astype(BF16).astype(F32)
+
+    def slope_of(value):
+        s = sigmoid(value)
+        return s * (1.0 + value * (1.0 - s))
+
+    def top_point(p, where):
+        return (cells(top, p, where) * slope_of(cells(part, p, where))).astype(BF16).astype(F32)
+
+    def delta_point(layer):
+        def point(p, where):
+            grad = cells(part, p, where).astype(BF16).astype(F32)
+            return (grad * slope_of(cells(pre.at[layer], p, where))).astype(BF16).astype(F32)
+
+        return point
+
+    def all_cells(body):
+        def one(p, carry):
+            body(p)
+            return carry
+
+        lax.fori_loop(0, 2, one, 0)
+
+    everywhere = slice(0, 8)
+
+    def whole_act(layer):
+        def body(p):
+            act = act_point(p, everywhere)
+            if layer < 2:
+                pre[layer, p] = part[p]
+                to_field(p, act)
+            else:
+                last[p] = act.reshape(64, 2, 8, 128)
+
+        all_cells(body)
+
+    def whole_delta(point):
+        def body(p):
+            delta = point(p, everywhere)
+            part[p] = delta
+            to_field(p, delta)
+
+        all_cells(body)
+
     for layer in range(LAYERS):
         if layer > 0:
-            faces_out(layer)
+            edge_faces(layer, act_point)
             send_faces(layer)
+            whole_act(layer - 1)
             inner(layer)
             conv_inner(layer, layer, True)
         if layer == 1:
@@ -500,37 +571,16 @@
             load_top()
         finish(layer, layer, True)
 
-        def forward(p, carry):
-            value = part[p]
-            slope = sigmoid(value)
-            act = (value * slope).astype(BF16).astype(F32)
-            if layer < 2:
-                pre[layer, p] = value
-                to_field(p, act)
-            else:
-                last[p] = act.reshape(64, 2, 8, 128)
-                slope = slope * (1.0 + value * (1.0 - slope))
-                delta = (top[p].reshape(8, 8, 16, 128) * slope).astype(BF16).astype(F32)
-                part[p] = delta
-                to_field(p, delta)
-            return carry
-
-        lax.fori_loop(0, 2, forward, 0)
+    write_out = pltpu.make_async_copy(held, out, store_sem.at[LAYERS])
 
     def store_out():
         def one(p, carry):
             for s in range(2):
-                out[2 * p + s] = last[p, :, s].reshape(512, 128).T[0:64].astype(BF16)
+                held[2 * p + s] = last[p, :, s].reshape(512, 128).T[0:64].astype(BF16)
             return carry
 
         lax.fori_loop(0, 2, one, 0)
-
-    def make_delta(layer, p, grad):
-        v = pre[layer, p]
-        s = sigmoid(v)
-        delta = (grad * (s * (1.0 + v * (1.0 - s)))).astype(BF16).astype(F32)
-        part[p] = delta
-        to_field(p, delta)
+        write_out.start()
 
     def spread_all():
         def one(p, carry):
@@ -541,8 +591,12 @@
 
     for layer in (2, 1):
         e = 5 - layer
-        faces_out(e)
+        point = top_point if layer == 2 else delta_point(layer)
+        edge_faces(e, point)
         send_faces(e)
+        if layer == 2:
+            whole_act(2)
+        whole_delta(point)
         spread_all()
         inner(e)
         conv_inner(e, layer, False)
@@ -550,11 +604,10 @@
         sum_0(layer)
         finish(e, layer, False)
 
-        def backward(p, carry):
-            make_delta(layer - 1, p, part[p].astype(BF16).astype(F32))
-            return carry
-
-        lax.fori_loop(0, 2, backward, 0)
+    def last_delta(p):
+        part[p] = delta_point(0)(p, everywhere)
+
+    all_cells(last_delta)
     spread_all()
     correlate(0)
     sum_0(0)
@@ -569,18 +622,38 @@
         sum_3(layer)
     for layer in range(LAYERS):
         sum_end(layer)
-
-
-def write_kernel(act, units, out, grads):
-    @pl.when(pl.program_id(0) == 0)
-    def _():
-        out[...] = act[...]
-
-    for unit, pair in enumerate(UNIT_KERNELS):
-        value = units[0, unit].astype(F32)
-        grads[0, pair[0]] = value[:, 0:64]
-        if len(pair) > 1:
-            grads[0, pair[1]] = swap_halves(value)[:, 0:64]
+        write_sum(layer).wait()
+    write_out.wait()
+
+
+def write_kernel(act, units, out, grads, held, units_in, wide, sems):
+    fetch_act = pltpu.make_async_copy(act, held, sems.at[0])
+    store_act = pltpu.make_async_copy(held, out, sems.at[1])
+    fetch = [
+        pltpu.make_async_copy(units.at[layer], units_in.at[layer], sems.at[2 + layer])
+        for layer in range(LAYERS)
+    ]
+    store = [
+        pltpu.make_async_copy(wide.at[layer], grads.at[layer], sems.at[2 + LAYERS + layer])
+        for layer in range(LAYERS)
+    ]
+    for copy in fetch:
+        copy.start()
+    fetch_act.start()
+    for layer in range(LAYERS):
+        fetch[layer].wait()
+        for unit, pair in enumerate(UNIT_KERNELS):
+            value = units_in[layer, unit].astype(F32)
+            wide[layer, pair[0]] = value[:, 0:64]
+            if len(pair) > 1:
+                wide[layer, pair[1]] = swap_halves(value)[:, 0:64]
+        store[layer].start()
+        if layer == 0:
+            fetch_act.wait()
+            store_act.start()
+    for copy in store:
+        copy.wait()
+    store_act.wait()
 
 
 def local(features, weights, cotangent, neighbours):
@@ -594,7 +667,7 @@
             jax.ShapeDtypeStruct((LAYERS, UNITS, 64, 128), BF16),
         ),
         in_specs=[vmem, hbm, hbm, pl.BlockSpec(memory_space=pltpu.SMEM)],
-        out_specs=(vmem, vmem),
+        out_specs=(hbm, hbm),
         scratch_shapes=[
             pltpu.SMEM((4 * 27 * 3,), jnp.int32),
             pltpu.VMEM((5, 64, 8, 128), F32),
@@ -607,10 +680,12 @@
             pltpu.VMEM((2, 8, 8, 16, 128), F32),
             pltpu.VMEM((4, 5, 8, 128), F32),
             pltpu.VMEM((2, 64, 2, 8, 128), F32),
-            pltpu.VMEM((2, 64, 2, 8, 128), F32),
+            pltpu.VMEM((2, 8, 8, 16, 128), F32),
             pltpu.VMEM((LAYERS, 27, 64, 64), BF16),
             pltpu.VMEM((4, 64, 512), BF16),
+            pltpu.VMEM((4, 64, 512), BF16),
             pltpu.SemaphoreType.DMA((2,)),
+            pltpu.SemaphoreType.DMA((LAYERS + 1,)),
             pltpu.SemaphoreType.DMA((5, 8)),
             pltpu.SemaphoreType.DMA((5, 8)),
             pltpu.SemaphoreType.DMA((LAYERS, 3)),
@@ -633,15 +708,14 @@
             jax.ShapeDtypeStruct((4, 64, 512), BF16),
             jax.ShapeDtypeStruct((LAYERS, 27, 64, 64), F32),
         ),
-        grid=(LAYERS,),
-        in_specs=[
-            pl.BlockSpec((4, 64, 512), lambda layer: (0, 0, 0)),
-            pl.BlockSpec((1, UNITS, 64, 128), lambda layer: (layer, 0, 0, 0)),
+        in_specs=[hbm, hbm],
+        out_specs=(hbm, hbm),
+        scratch_shapes=[
+            pltpu.VMEM((4, 64, 512), BF16),
+            pltpu.VMEM((LAYERS, UNITS, 64, 128), BF16),
+            pltpu.VMEM((LAYERS, 27, 64, 64), F32),
+            pltpu.SemaphoreType.DMA((2 + 2 * LAYERS,)),
         ],
-        out_specs=(
-            pl.BlockSpec((4, 64, 512), lambda layer: (0, 0, 0)),
-            pl.BlockSpec((1, 27, 64, 64), lambda layer: (layer, 0, 0, 0)),
-        ),
         compiler_params=pltpu.CompilerParams(vmem_limit_bytes=56 * 1024 * 1024),
     )(act, units)
 

time: 61.5 us -> 59.7 us (0.971)
  Pallas kernels: 60.7 us -> 58.7 us
    pallas_call x1, Pallas kernels: 57.2 us -> 56 us  [local(): pl.pallas_call(functools.partial(kernel, rows, cols, 1.0 / math.sqrt(4 *...]
    pallas_call x1, Pallas kernels: 3.49 us -> 2.72 us  [local(): pl.pallas_call(write_kernel, out_shape=(jax.ShapeDtypeStruct((4, 64, 512)...]
where the time goes in v7:
time: 59.7 us; the launch traced here: 59.5 us
  Pallas kernels  58.7 us (98%)
  between operations  0.8 us (1%)
    pallas_call x1, Pallas kernels, local(): pl.pallas_call(functools.partial(kernel, rows, cols, 1.0 / math.sqrt(4 *...  56 us
    pallas_call x1, Pallas kernels, local(): pl.pallas_call(write_kernel, out_shape=(jax.ShapeDtypeStruct((4, 64, 512)...  2.72 us

profile of v7, /device:TPU:1, one launch (start us, length us, event | category | flops | bytes accessed | tf_op | source)
XLA Modules:
  0.0 59.5 jit_solution(399303555946808895)
XLA Ops:
  0.6 56.0 %shard_map.59 = (bf16[4,64,512]{2,1,0:T(8,128)(2,1)}, bf16[3,14,64,128]{3,2,1,0:T(8,128)(2,1)}) custom-call(bf16[4,64,512]{2,1,0:T(8,128)(2,1)} %feat.1, bf16[3,27,64,64]{3,2,1,0:T(8,128)(2,1)} %w_hbm.1, bf16[4,64,512]{2,1,0:T(8,128)(2,1)} %cot_hbm.1, s32[4,27]{1,0:T(4,128)} %nbr.1), custom_call_target="tpu_custom_call" | custom-call | tf_op jit(solution)/shard_map/pallas_call | solution.py:663
  56.6 2.7 %shard_map.60 = (bf16[4,64,512]{2,1,0:T(8,128)(2,1)}, f32[3,27,64,64]{3,2,1,0:T(8,128)}) custom-call(bf16[4,64,512]{2,1,0:T(8,128)(2,1)} %get-tuple-element.4.act, bf16[3,14,64,128]{3,2,1,0:T(8,128)(2,1)} %get-tuple-element.5.units), custom_call_target="tpu_custom_call" | custom-call | tf_op jit(solution)/shard_map/pallas_call | solution.py:705

commit v8 on v7

--- a/solution.py
+++ b/solution.py
@@ -326,15 +326,26 @@
             for p in range(2):
                 part[p, :, y] += over_dx(acc[p])
 
+    def conv_corners(z, layer, forward):
+        for cell, dy, y in ((0, 0, 0), (9, 2, 7)):
+            lines = jnp.concatenate(
+                [zp[z, p, x, cell] for x in (0, 9) for p in range(2)], axis=0
+            )
+            acc = multiply(lines, layer, forward, dy).reshape(2, 2, 16, 256)
+            for p in range(2):
+                part[p, 0, y] += acc[0, p, :, 0:128]
+                part[p, 7, y] += acc[1, p, :, 128:256]
+
     def finish(e, layer, forward):
         arrive(e, 6, 8)
         halo_x(e, e)
+        conv_planes(e, layer, forward)
         arrive(e, 4, 6)
         halo_y(e, e)
         conv_lines(e, layer, forward)
         arrive(e, 0, 4)
         halo_edges(e, e)
-        conv_planes(e, layer, forward)
+        conv_corners(e, layer, forward)
 
     def to_field(p, value):
         value = value.reshape(64, 2, 8, 128)
@@ -494,6 +505,8 @@
             for p in range(2):
                 for y in (0, 9):
                     zp[e, p, 1:9, y] = jnp.zeros((8, 16, 256), BF16)
+                    for x in (0, 9):
+                        zp[e, p, x, y] = jnp.zeros((16, 256), BF16)
         for q in range(4):
             corner[q, 4] = jnp.zeros((8, 128), F32)
 

time: 59.7 us -> 59.5 us (level)
  no operation moved by 1% of the time
where the time goes in v8:
time: 59.5 us; the launch traced here: 59.3 us
  Pallas kernels  58.5 us (98%)
  between operations  0.8 us (1%)
    pallas_call x1, Pallas kernels, local(): pl.pallas_call(functools.partial(kernel, rows, cols, 1.0 / math.sqrt(4 *...  55.8 us
    pallas_call x1, Pallas kernels, local(): pl.pallas_call(write_kernel, out_shape=(jax.ShapeDtypeStruct((4, 64, 512)...  2.72 us

profile of v8, /device:TPU:1, one launch (start us, length us, event | category | flops | bytes accessed | tf_op | source)
XLA Modules:
  0.0 59.3 jit_solution(1808610546864406443)
XLA Ops:
  0.6 55.8 %shard_map.59 = (bf16[4,64,512]{2,1,0:T(8,128)(2,1)}, bf16[3,14,64,128]{3,2,1,0:T(8,128)(2,1)}) custom-call(bf16[4,64,512]{2,1,0:T(8,128)(2,1)} %feat.1, bf16[3,27,64,64]{3,2,1,0:T(8,128)(2,1)} %w_hbm.1, bf16[4,64,512]{2,1,0:T(8,128)(2,1)} %cot_hbm.1, s32[4,27]{1,0:T(4,128)} %nbr.1), custom_call_target="tpu_custom_call" | custom-call | tf_op jit(solution)/shard_map/pallas_call | solution.py:676
  56.4 2.7 %shard_map.60 = (bf16[4,64,512]{2,1,0:T(8,128)(2,1)}, f32[3,27,64,64]{3,2,1,0:T(8,128)}) custom-call(bf16[4,64,512]{2,1,0:T(8,128)(2,1)} %get-tuple-element.4.act, bf16[3,14,64,128]{3,2,1,0:T(8,128)(2,1)} %get-tuple-element.5.units), custom_call_target="tpu_custom_call" | custom-call | tf_op jit(solution)/shard_map/pallas_call | solution.py:718
